TPU v7x, 32 devices: a whole 2x2x4 slice. The times are simulated.
32 devices in a mesh: section: 2 (over core), dp: 16 (over z, y, x).
Axes of the slice: x: 2, y: 2, z: 4, core: 2. Of those that a mesh axis runs over, the one named last changes fastest.
Arguments:
- enc_in: bfloat16 [32, 512, 768], P('dp'), may hold values from -6 to 6
- dec_in: bfloat16 [128, 768], P('dp'), may hold values from -6 to 6
- segment: int32 [32, 512], P('dp'), may hold values from 0 to 3, never falling along the last dimension, each value on 1 to 256 neighbouring positions
- d_out: bfloat16 [128, 768], P('dp'), may hold values from -6 to 6
- attn_gain: bfloat16 [2, 768], P('section', 'dp'), may hold values from 0.5 to 1.5
- w_query: bfloat16 [2, 768, 768], P('section', 'dp'), may hold values from -0.0390625 to 0.0390625
- w_key: bfloat16 [2, 768, 768], P('section', 'dp'), may hold values from -0.21875 to 0.21875
- w_value: bfloat16 [2, 768, 768], P('section', 'dp'), may hold values from -0.21875 to 0.21875
- w_out: bfloat16 [2, 768, 768], P('section', 'dp'), may hold values from -0.625 to 0.625
- ffn_gain: bfloat16 [2, 768], P('section', 'dp'), may hold values from 0.5 to 1.5
- w_in: bfloat16 [2, 768, 3072], P('section', 'dp'), may hold values from -0.21875 to 0.21875
- w_back: bfloat16 [2, 3072, 768], P('section', 'dp'), may hold values from -0.109375 to 0.109375
- self_gain: bfloat16 [768], P(('section', 'dp')), may hold values from 0.5 to 1.5
- self_value: bfloat16 [768, 768], P(('section', 'dp')), may hold values from -0.21875 to 0.21875
- self_out: bfloat16 [768, 768], P(('section', 'dp')), may hold values from -0.21875 to 0.21875
- rel_table: float32 [32, 12], replicated, may hold values from -4 to 4
Outputs:
- dec_out: bfloat16 [128, 768], P('dp', 'section')
- enc_in_grad: bfloat16 [32, 512, 768], P('dp', None, 'section')
- dec_in_grad: bfloat16 [128, 768], P('dp', 'section')
- g_attn_gain: float32 [2, 768], P('section', 'dp')
- g_w_query: float32 [2, 768, 768], P('section', 'dp')
- g_w_key: float32 [2, 768, 768], P('section', 'dp')
- g_w_value: float32 [2, 768, 768], P('section', 'dp')
- g_w_out: float32 [2, 768, 768], P('section', 'dp')
- g_ffn_gain: float32 [2, 768], P('section', 'dp')
- g_w_in: float32 [2, 768, 3072], P('section', 'dp')
- g_w_back: float32 [2, 3072, 768], P('section', 'dp')
- g_self_gain: float32 [768], P(('section', 'dp'))
- g_self_value: float32 [768, 768], P(('section', 'dp'))
- g_self_out: float32 [768, 768], P(('section', 'dp'))
- g_rel_table: float32 [32, 12], replicated
Inputs may be any that keep to these rules, and one draw needn't show every extreme that they name: `segment`: in each row the pair numbers never fall along the tokens, each of the 4 numbers covers 1 to 256 tokens, and one covers exactly 256.
All inputs are finite; a program needn't handle non-finite values.
Results may differ from a plain program's by a relative error of at most 0.025.
The roundings to bfloat16 on the way count: a program that leaves them out, or rounds other values in their place, can miss the bound.
Values may be sent and summed in bfloat16 or wider, within the bound.
No kernel may reach another device: no remote copies, remote signals or barrier semaphores. Data moves between devices by JAX's collectives and lax.ppermute only.
A program may use at most 448 MiB of HBM per device.

v0:
```python
import functools

import jax
import jax.numpy as jnp
import numpy as np
from jax import lax
from jax.experimental import pallas as pl
from jax.experimental.pallas import tpu as pltpu
from jax.sharding import PartitionSpec as P

D = 768
HEADS = 12
HEAD_DIM = 64
FF = 3072
BUCKETS = 32
MAX_DIST = 128
ROW_LEN = 512
SEGS = 4
GROUP = 48
GROUPS = D // GROUP
X, Y, Z0, Z1 = 0, 1, 2, 3
TILE = 128
EPS = 1e-06
MASKED = -1000000000.0
BF = jnp.bfloat16
F32 = jnp.float32
SPEED = 0.25
VMEM_LIMIT = 58 * 1024 * 1024


def bucket_of(offset):
    half, exact = BUCKETS // 2, BUCKETS // 4
    exponent, growth = half - exact, MAX_DIST // exact
    distance = abs(offset)
    if distance < exact:
        level = distance
    else:
        k = 0
        while k < exponent and exact**exponent * growth ** (k + 1) <= distance**exponent:
            k += 1
        level = min(exact + k, half - 1)
    return (half if offset > 0 else 0) + level


def window_onehots():
    table = np.zeros((2, 3, 2 * TILE, BUCKETS), np.float32)
    for d in range(3):
        for t in range(2 * TILE):
            table[0, d, t, bucket_of(TILE * (d - 1) - TILE + t)] = 1.0
            table[1, d, t, bucket_of(TILE * (d - 1) + TILE - t)] = 1.0
    return table


def diagonal_onehots():
    table = np.zeros((5, 2 * TILE, BUCKETS), np.float32)
    table[1:4] = window_onehots()[1]
    table[0, :, bucket_of(-TILE - 1)] = 1.0
    table[4, :, bucket_of(TILE + 1)] = 1.0
    return table


def across(value):
    return lax.ppermute(value, "section", [(0, 1), (1, 0)])


def along(value, bit):
    count = lax.axis_size("dp")
    return lax.ppermute(value, "dp", [(i, i ^ (1 << bit)) for i in range(count)])


def bit_of(index, bit):
    return lax.rem(lax.div(index, 1 << bit), 2)


def low_bits(rows):
    count = 0
    while rows < GROUP:
        rows *= 2
        count += 1
    return count


def filled(piece, pre, chip, axis):
    for bit in range(pre):
        other = along(piece, bit)
        upper = bit_of(chip, bit) == 1
        first = jnp.where(upper, other, piece)
        second = jnp.where(upper, piece, other)
        piece = jnp.concatenate([first, second], axis=axis)
    return piece


def narrowed(total, pre, chip):
    for bit in reversed(range(pre)):
        length = total.shape[0] // 2
        upper = bit_of(chip, bit)
        kept = lax.dynamic_slice_in_dim(total, upper * length, length, 0)
        sent = lax.dynamic_slice_in_dim(total, (1 - upper) * length, length, 0)
        total = added(kept, along(sent.astype(BF), bit), F32)
    return total


def phase(*things):
    tree = [thing.arrays() if isinstance(thing, (Chain, Sum)) else thing for thing in things]
    out = []
    for thing, value in zip(things, lax.optimization_barrier(tree)):
        if isinstance(thing, (Chain, Sum)):
            thing.replace(value)
        else:
            out.append(value)
    return out[0] if len(out) == 1 else out


class Chain:
    def __init__(self, parts, ids, pre):
        self.parts, self.ids, self.pre = parts, ids, pre

    def arrays(self):
        return list(self.parts)

    def replace(self, values):
        self.parts = values

    def split(self, at):
        cut = [[part[:, :at] for part in self.parts], [part[:, at:] for part in self.parts]]
        return [Chain(parts, self.ids, self.pre) for parts in cut]

    def step(self, bit):
        held = self.parts[0] if len(self.parts) == 1 else jnp.concatenate(self.parts, axis=0)
        self.parts = [held, along(held, bit + self.pre)]
        self.old_ids = self.ids
        self.ids = self.ids + [g ^ (1 << bit) for g in self.ids]

    def sets(self, others):
        first, last = self.old_ids, self.ids[len(self.old_ids) :]
        return [(self.parts[0], first, 0), (self.parts[1], last, 0), (others[0], first, 1), (others[1], last, 1)]


def added(left, right, kind=BF):
    return (left.astype(F32) + right.astype(F32)).astype(kind)


class Sum:
    def __init__(self, keep, send, pre):
        self.mine, self.other, self.pre, self.fresh = keep, send, pre, True

    def arrays(self):
        return [self.mine, self.other]

    def replace(self, values):
        self.mine, self.other = values

    def step(self, bit):
        if self.fresh:
            send, self.fresh = self.other, False
        else:
            half = self.mine.shape[0] // 2
            send = added(self.mine[half:], self.other[half:])
            self.mine = added(self.mine[:half], self.other[:half])
        self.other = along(send, bit + self.pre)

    def total(self):
        return added(self.mine[0], self.other[0], F32)


def merged(sums):
    one = Sum(
        jnp.concatenate([part.mine for part in sums], axis=1),
        jnp.concatenate([part.other for part in sums], axis=1),
        sums[0].pre,
    )
    one.fresh = False
    return one


def nn(a, b):
    return lax.dot_general(a, b, (((1,), (0,)), ((), ())), preferred_element_type=F32)


def nt(a, b):
    return lax.dot_general(a, b, (((1,), (1,)), ((), ())), preferred_element_type=F32)


def tn(a, b):
    return lax.dot_general(a, b, (((0,), (0,)), ((), ())), preferred_element_type=F32)


def rms(v, gain):
    return v * lax.rsqrt(jnp.mean(v * v, axis=-1, keepdims=True) + EPS) * gain


def rms_back(v, gain, dy):
    r = lax.rsqrt(jnp.mean(v * v, axis=-1, keepdims=True) + EPS)
    dgain = jnp.sum(dy * v * r, axis=0, keepdims=True)
    dyg = dy * gain
    dv = r * dyg - v * (r * r * r) * jnp.mean(v * dyg, axis=-1, keepdims=True)
    return dv, dgain


def gelu_both(u):
    c = 0.7978845608028654
    t = jnp.tanh(c * (u + 0.044715 * u * u * u))
    value = 0.5 * u * (1.0 + t)
    slope = 0.5 * (1.0 + t) + (0.5 * c) * u * (1.0 - t * t) * (1.0 + 3 * 0.044715 * u * u)
    return value, slope


def square_row(b):
    return lambda core, g: (core * 2 + b) * D + GROUP * g


def back_row(b):
    return lambda core, g: 4 * GROUP * g + GROUP * (2 * core + b)


def in_items(first):
    return [(first + GROUP * b, GROUP, square_row(b), lambda core, g, b=b: 2 * core + b) for b in range(2)]


def in_sources(a_sets, b_sets):
    cut = 2 * GROUP // 3
    later = lambda core, g: square_row(1)(core, g) + cut
    block = lambda core, g: 2 * core + 1
    return [
        (a_sets, [(0, GROUP, square_row(0), lambda core, g: 2 * core), (GROUP, cut, square_row(1), block)]),
        (b_sets, [(GROUP, GROUP - cut, later, block)]),
    ]


def back_sources(b_sets, shared, first, got):
    quarter = lambda core, g: g // 4
    return [
        (b_sets, [(0, GROUP, back_row(0), quarter)]),
        ([(shared, None, 0)], [(first, GROUP, back_row(1), quarter)]),
        ([(got, None, 1)], [(0, GROUP, back_row(1), quarter)]),
    ]


def arrays_of(sources):
    return [part for sets, items in sources for part, ids, other in sets]


def start_sources(meta, refs, sources, dst, sems):
    at = 0
    for sets, items in sources:
        plan = [(ids, other) for part, ids, other in sets]
        start_fetch(meta, refs[at : at + len(plan)], plan, items, dst, sems)
        at += len(plan)


def start_fetch(meta, refs, plan, items, dst, sem, only=None):
    if only is not None:
        for other in range(2):
            part = [(ref, entry) for ref, entry in zip(refs, plan) if entry[1] == other]

            @pl.when(jnp.bitwise_xor(meta[1], other) == only)
            def _():
                start_fetch(meta, [r for r, e in part], [e for r, e in part], items, dst, sem)

        return
    me, core = meta[0], meta[1]
    for first, count, row_of, *sem_of in items:
        for ref, (ids, other) in zip(refs, plan):
            source = 1 - core if other else core
            for slot in range(ref.shape[0]):
                group = jnp.int32(slot) if ids is None else jnp.bitwise_xor(me, ids[slot])
                off = pl.multiple_of(row_of(source, group), 16)
                at = sem.at[sem_of[0](source, group)] if sem_of else sem
                pltpu.make_async_copy(ref.at[slot, pl.ds(first, count)], dst.at[pl.ds(off, count)], at).start()


def drain(ref, sem):
    pltpu.make_async_copy(ref, ref, sem).wait()


def slot_of(meta, group, b):
    rel = jnp.bitwise_xor(meta[0], group)
    x, y, z0, z1 = [jnp.bitwise_and(rel // (1 << bit), 1) for bit in range(4)]
    return (8 * y + 4 * x if b == 0 else 8 * x + 4 * y) + 2 * z0 + z1


def start_store(meta, src, group, b, keep, send, sem, rows=slice(None), cols=slice(None)):
    slot = slot_of(meta, group, b)
    at = (rows, cols)

    @pl.when(slot < GROUPS // 2)
    def _():
        pltpu.make_async_copy(src, keep.at[(slot,) + at], sem).start()

    @pl.when(slot >= GROUPS // 2)
    def _():
        pltpu.make_async_copy(src, send.at[(slot - GROUPS // 2,) + at], sem).start()


def head_lanes(h):
    lane = lax.broadcasted_iota(jnp.int32, (1, D), 1)
    return (lane >= h * HEAD_DIM) & (lane < (h + 1) * HEAD_DIM)


def pair_lanes(hh):
    lane = lax.broadcasted_iota(jnp.int32, (1, TILE), 1)
    return (lane < HEAD_DIM) if hh == 0 else (lane >= HEAD_DIM)


def masked(value, lanes):
    return jnp.where(lanes, value, jnp.zeros_like(value))


def fill_bias(window_ref, tiles, transposed):
    part = 1 if transposed else 0

    def one(h, carry):
        for d in range(3):
            row = jnp.broadcast_to(window_ref[h, pl.ds(part * 3 + d, 1), :], (TILE, 2 * TILE))
            rolled = pltpu.roll(row, TILE, 1, stride=1, stride_axis=0)
            tiles[h, d + 1] = rolled[:, :TILE]
        low = window_ref[h, pl.ds(0, 1), pl.ds(0, 1)]
        high = window_ref[h, pl.ds(2, 1), pl.ds(2 * TILE - 1, 1)]
        tiles[h, 0] = jnp.broadcast_to(low, (TILE, TILE))
        tiles[h, 4] = jnp.broadcast_to(high, (TILE, TILE))
        return carry

    lax.fori_loop(0, HEADS, one, 0)


def spec(space):
    return space if isinstance(space, pl.BlockSpec) else pl.BlockSpec(memory_space=space)


def call(body, name, ins, spaces, outs, out_spaces, scratch, us, aliases={}, grid=()):
    if grid:
        specs = {
            "grid_spec": pltpu.PrefetchScalarGridSpec(
                num_scalar_prefetch=1,
                grid=grid,
                in_specs=[spec(s) for s in spaces[1:]],
                out_specs=[spec(s) for s in out_spaces],
                scratch_shapes=scratch,
            )
        }
    else:
        specs = {
            "in_specs": [spec(s) for s in spaces],
            "out_specs": [spec(s) for s in out_spaces],
            "scratch_shapes": scratch,
        }
    return pl.pallas_call(
        body,
        name=name,
        out_shape=[jax.ShapeDtypeStruct(s, k) for s, k in outs],
        input_output_aliases=aliases,
        compiler_params=pltpu.CompilerParams(vmem_limit_bytes=VMEM_LIMIT),
        cost_estimate=pl.CostEstimate(flops=int(us * SPEED * 1.1e9), bytes_accessed=int(us * SPEED * 1e6), transcendentals=0),
        **specs,
    )(*ins)


VM, SM, ANY = pltpu.VMEM, pltpu.SMEM, pl.ANY


def plan_of(sets):
    return [part for part, ids, other in sets], [(ids, other) for part, ids, other in sets]


def enc_attention(meta, x, gains, segr, segc, windows, a_sets, b_sets):
    a_arrays, a_plan = plan_of(a_sets)
    b_arrays, b_plan = plan_of(b_sets)
    n = len(a_arrays)

    def body(meta, x, gains, segr, segc, windows, *rest):
        a_parts, b_parts, rest = rest[:n], rest[n : 2 * n], rest[2 * n :]
        n1, q, k, v, c, h1, n2, lse, w, tiles, lcol, sems = rest
        start_fetch(meta, a_parts, a_plan, [(0, GROUP, square_row(0))], w, sems.at[0])
        start_fetch(meta, b_parts, b_plan, [(0, GROUP, square_row(1))], w, sems.at[0])
        fill_bias(windows, tiles, False)
        xf = x[...].astype(F32)
        n1[...] = rms(xf, gains[0:1, :]).astype(BF)
        drain(w, sems.at[0])
        for ref, at in ((q, 0), (k, 2), (v, 3)):
            ref[...] = nn(n1[...], w[at * D : (at + 1) * D, :]).astype(BF)
        lane = lax.broadcasted_iota(jnp.int32, (1, TILE), 1)
        lcol[...] = jnp.zeros_like(lcol)

        def pair(pr, carry):
            cols = pl.ds(pl.multiple_of(pr * TILE, TILE), TILE)
            kp, vp = k[:, cols], v[:, cols]
            for ib in range(ROW_LEN // TILE):
                rows = slice(ib * TILE, (ib + 1) * TILE)
                same = segc[rows, :] == segr[...]
                qp = q[rows, cols]
                total = jnp.zeros((TILE, TILE), F32)
                for hh in range(2):
                    h = 2 * pr + hh
                    lanes = pair_lanes(hh)
                    bias = jnp.concatenate(
                        [tiles[h, min(max(jb - ib, -2), 2) + 2] for jb in range(ROW_LEN // TILE)], axis=1
                    )
                    s = jnp.where(same, nt(masked(qp, lanes), kp) + bias, MASKED)
                    top = jnp.max(s, axis=-1, keepdims=True)
                    ex = jnp.exp(s - top)
                    tot = jnp.sum(ex, axis=-1, keepdims=True)
                    p = (ex * (1.0 / tot)).astype(BF)
                    total = total + nn(p, masked(vp, lanes))
                    lcol[rows, :] = jnp.where(lane == h, top + jnp.log(tot), lcol[rows, :])
                c[rows, cols] = total.astype(BF)
            return carry

        lax.fori_loop(0, HEADS // 2, pair, 0)
        lse[...] = lcol[...].T
        res = x[...].astype(F32) + nn(c[...], w[D : 2 * D, :])
        h1[...] = res
        n2[...] = rms(res, gains[1:2, :]).astype(BF)

    rows = (ROW_LEN, D)
    return call(
        body, "enc_attention", [meta, x, gains, segr, segc, windows, *a_arrays, *b_arrays],
        [SM, VM, VM, VM, VM, VM] + [ANY] * (2 * n),
        [(rows, BF)] * 5 + [(rows, F32), (rows, BF), ((TILE, ROW_LEN), F32), ], [VM] * 8,
        [pltpu.VMEM((4 * D, D), BF), pltpu.VMEM((HEADS, 5, TILE, TILE), F32), pltpu.VMEM((ROW_LEN, TILE), F32), pltpu.SemaphoreType.DMA((2,))],
        us=20,
    )


PART = (GROUPS // 2, GROUP, D)
WIDE_PART = (GROUPS // 2, 2 * GROUP, D)
BLOCKS = FF // D


def enc_ffn(meta, h1, n2, w_in_from, w_back_from):
    in_arrays, back_arrays = arrays_of(w_in_from), arrays_of(w_back_from)
    n, m = len(in_arrays), len(back_arrays)

    def body(meta, h1, n2, *rest):
        ins, backs, rest = rest[:n], rest[n : n + m], rest[n + m :]
        f, slope, e, w_in, w_back, acc, sems = rest
        start_sources(meta, ins, w_in_from, w_in, sems)
        start_sources(meta, backs, w_back_from, w_back, sems.at[pl.ds(4, 4)])
        acc[...] = h1[...]

        def block(b, carry):
            rows = pl.ds(pl.multiple_of(b * D, D), D)

            drain(w_in.at[rows], sems.at[b])
            value, grad = gelu_both(nn(n2[...], w_in[rows, :]))
            fb = value.astype(BF)
            f[:, rows] = fb
            slope[:, rows] = grad.astype(BF)
            drain(w_back.at[rows], sems.at[4 + b])
            acc[...] += nn(fb, w_back[rows, :])
            return carry

        lax.fori_loop(0, FF // D, block, 0)
        e[...] = acc[...].astype(BF)

    return call(
        body, "enc_ffn", [meta, h1, n2, *in_arrays, *back_arrays], [SM, VM, VM] + [ANY] * (n + m),
        [((ROW_LEN, FF), BF), ((ROW_LEN, FF), BF), ((ROW_LEN, D), BF)], [VM] * 3,
        [pltpu.VMEM((FF, D), BF), pltpu.VMEM((FF, D), BF), pltpu.VMEM((ROW_LEN, D), F32),
         pltpu.SemaphoreType.DMA((8,))],
        us=15,
    )


def enc_hidden_grad(meta, de, slope, w_back_from):
    arrays = arrays_of(w_back_from)
    n = len(arrays)

    def body(meta, de, slope, *rest):
        parts, rest = rest[:n], rest[n:]
        du, other, w, sems = rest
        b = pl.program_id(0)

        @pl.when(b == 0)
        def _():
            start_sources(meta, parts, w_back_from, w, sems)

        rows = pl.ds(pl.multiple_of(b * D, D), D)
        drain(w.at[rows], sems.at[b])
        value = (slope[...].astype(F32) * nt(de[...], w[rows, :])).astype(BF)
        du[...] = value

        @pl.when(meta[1] != b // 2)
        def _():
            other[:, pl.ds(pl.multiple_of(b % 2 * D, D), D)] = value

    block = pl.BlockSpec((ROW_LEN, D), lambda b, meta: (0, b))
    return call(
        body, "enc_hidden_grad", [meta, de, slope, *arrays], [SM, VM, block] + [ANY] * n,
        [((ROW_LEN, FF), BF), ((ROW_LEN, FF // 2), BF)], [block, VM],
        [pltpu.VMEM((FF, D), BF), pltpu.SemaphoreType.DMA((4,))],
        us=8, grid=(BLOCKS,),
    )


def enc_w_back_grad(meta, de, de_got, f, f_got):
    half = D // 2

    def body(meta, de, de_got, f, f_got, keep_a, send_a, keep_b, send_b, mine, buf, sems):
        mine[...] = de[:, pl.ds(pl.multiple_of(meta[1] * half, TILE), half)]
        for b in range(FF // D):
            cols = slice(b * D, (b + 1) * D)
            at = b % 2
            if b >= 2:
                drain(buf.at[at], sems.at[at])
            buf[at] = (tn(f[:, cols], mine[...]) + tn(f_got[:, cols], de_got[...])).astype(BF)
            for k in range(D // GROUP):
                group, piece = b * (D // GROUP // 4) + k // 4, k % 4
                keep, send = (keep_a, send_a) if piece < 2 else (keep_b, send_b)
                start_store(meta, buf.at[at, pl.ds(k * GROUP, GROUP)], group, piece // 2, keep, send, sems.at[at],
                            cols=pl.ds((piece % 2) * half, half))
        drain(buf.at[0], sems.at[0])
        drain(buf.at[1], sems.at[1])

    return call(
        body, "enc_w_back_grad", [meta, de, de_got, f, f_got], [SM] + [VM] * 4,
        [(PART, BF)] * 4, [ANY] * 4,
        [pltpu.VMEM((ROW_LEN, half), BF), pltpu.VMEM((2, D, half), BF), pltpu.SemaphoreType.DMA((2,))],
        us=7,
    )


def enc_w_in_grad(meta, du, du_got, n2, n2_got, wide_keep, wide_send):
    def body(meta, du, du_got, n2, n2_got, wide_keep, wide_send, keep_a, send_a, keep_b, send_b, buf, sems):
        for b in range(2):
            cols = pl.ds(pl.multiple_of(meta[1] * (FF // 2) + b * D, TILE), D)
            buf[b] = (tn(n2[...], du[:, cols]) + tn(n2_got[...], du_got[:, b * D : (b + 1) * D])).astype(BF)
            keep, send = (keep_a, send_a) if b == 0 else (keep_b, send_b)
            for g in range(GROUPS):
                rows = pl.ds(0, GROUP)
                start_store(meta, buf.at[b, pl.ds(g * GROUP, GROUP)], g, b, keep, send, sems.at[b], rows)
        drain(buf.at[0], sems.at[0])
        drain(buf.at[1], sems.at[1])

    return call(
        body, "enc_w_in_grad", [meta, du, du_got, n2, n2_got, wide_keep, wide_send], [SM] + [VM] * 4 + [ANY] * 2,
        [(WIDE_PART, BF), (WIDE_PART, BF), (PART, BF), (PART, BF)], [ANY] * 4,
        [pltpu.VMEM((2, D, D), BF), pltpu.SemaphoreType.DMA((2,))],
        us=7, aliases={5: 0, 6: 1},
    )


def enc_ffn_back(meta, du, h1, de, gains, w_in_from):
    arrays = arrays_of(w_in_from)
    n = len(arrays)

    def body(meta, du, h1, de, gains, *rest):
        parts, rest = rest[:n], rest[n:]
        dh1, da, dgain, w, acc, sems = rest
        start_sources(meta, parts, w_in_from, w, sems)
        for k, b in enumerate((0, 2, 1, 3)):
            cols = slice(b * D, (b + 1) * D)
            drain(w.at[cols], sems.at[b])
            part = nt(du[:, cols], w[cols, :])
            acc[...] = part if k == 0 else acc[...] + part
        dv, dg = rms_back(h1[...], gains[1:2, :], acc[...])
        total = de[...].astype(F32) + dv
        dh1[...] = total
        da[...] = total.astype(BF)
        dgain[...] = dg

    rows = (ROW_LEN, D)
    return call(
        body, "enc_ffn_back", [meta, du, h1, de, gains, *arrays], [SM, VM, VM, VM, VM] + [ANY] * n,
        [(rows, F32), (rows, BF), ((1, D), F32)], [VM, VM, VM],
        [pltpu.VMEM((FF, D), BF), pltpu.VMEM(rows, F32), pltpu.SemaphoreType.DMA((4,))],
        us=8,
    )


def enc_attention_back(meta, da, q, k, v, lse, segr, segc, windows, sets):
    arrays, plan = plan_of(sets)
    n = len(arrays)
    wide = 2 * TILE

    def body(meta, da, q, k, v, lse, segr, segc, windows, *rest):
        parts, rest = rest[:n], rest[n:]
        dq, dk, dv, diag, other, w, dc, tiles, sums, kacc, vacc, sem = rest
        start_fetch(meta, parts, plan, [(0, GROUP, lambda core, g: GROUP * g)], w, sem, only=0)
        fill_bias(windows, tiles, True)
        drain(w, sem)
        dc[...] = nt(da[...], w[...]).astype(BF)
        row = lax.broadcasted_iota(jnp.int32, (TILE, TILE), 0)
        col = lax.broadcasted_iota(jnp.int32, (TILE, TILE), 1)
        flip = (row + col == TILE - 1).astype(F32)

        def pair(pr, carry):
            cols = pl.ds(pl.multiple_of(pr * TILE, TILE), TILE)
            for hh in range(2):
                h = 2 * pr + hh
                lanes = pair_lanes(hh)
                km, vm = masked(k[:, cols], lanes), masked(v[:, cols], lanes)
                sums[...] = jnp.zeros_like(sums)
                for ib in range(ROW_LEN // wide):
                    rows = slice(ib * wide, (ib + 1) * wide)
                    same = segc[...] == segr[:, rows]
                    qp, dcp = q[rows, cols], dc[rows, cols]
                    bias = jnp.concatenate([
                        jnp.concatenate([
                            tiles[h, min(max(jb - (2 * ib + i), -2), 2) + 2] for i in range(2)
                        ], axis=1) for jb in range(ROW_LEN // TILE)
                    ], axis=0)
                    s = jnp.where(same, nt(km, qp) + bias, MASKED)
                    prob = jnp.exp(s - lse[pl.ds(h, 1), rows])
                    dprob = nt(vm, dcp)
                    inner = jnp.sum(prob * dprob, axis=0, keepdims=True)
                    ds = (prob * (dprob - inner)).astype(BF)
                    dvp = nn(prob.astype(BF), masked(dcp, lanes))
                    dkp = nn(ds, masked(qp, lanes))
                    dqp = tn(ds, km)
                    if hh == 0 and ib == 0:
                        vacc[...], kacc[...] = dvp, dkp
                    else:
                        vacc[...] += dvp
                        kacc[...] += dkp
                    if hh == 0:
                        dq[rows, cols] = dqp.astype(BF)
                    else:
                        dq[rows, cols] = dq[rows, cols] + dqp.astype(BF)
                    for jb in range(ROW_LEN // TILE):
                        for i in range(2):
                            d = min(max(jb - (2 * ib + i), -2), 2) + 2
                            sums[d] += ds[jb * TILE : (jb + 1) * TILE, i * TILE : (i + 1) * TILE].astype(F32)
                for d in range(5):
                    if d in (0, 4):
                        line = jnp.sum(sums[d], axis=0, keepdims=True)
                        diag[h, d : d + 1, :] = jnp.concatenate([line, jnp.zeros_like(line)], axis=1)
                    else:
                        turned = lax.dot_general(
                            flip, sums[d], (((1,), (0,)), ((), ())),
                            precision=lax.Precision.HIGHEST, preferred_element_type=F32,
                        )
                        wider = jnp.concatenate([turned, jnp.zeros_like(turned)], axis=1)
                        rolled = pltpu.roll(wider, 1, 1, stride=1, stride_axis=0)
                        diag[h, d : d + 1, :] = jnp.sum(rolled, axis=0, keepdims=True)
            dk[:, cols] = kacc[...].astype(BF)
            dv[:, cols] = vacc[...].astype(BF)
            return carry

        lax.fori_loop(0, HEADS // 2, pair, 0)

        @pl.when(meta[1] == 0)
        def _():
            other[0] = dk[...]
            other[1] = dv[...]

        @pl.when(meta[1] != 0)
        def _():
            other[0] = dq[...]
            other[1] = da[...]

    rows = (ROW_LEN, D)
    return call(
        body, "enc_attention_back", [meta, da, q, k, v, lse, segr, segc, windows, *arrays],
        [SM] + [VM] * 8 + [ANY] * n,
        [(rows, BF), (rows, BF), (rows, BF), ((HEADS, 5, 2 * TILE), F32), ((2,) + rows, BF)], [VM] * 5,
        [pltpu.VMEM((D, D), BF), pltpu.VMEM(rows, BF), pltpu.VMEM((HEADS, 5, TILE, TILE), F32),
         pltpu.VMEM((5, TILE, TILE), F32), pltpu.VMEM((ROW_LEN, TILE), F32), pltpu.VMEM((ROW_LEN, TILE), F32),
         pltpu.SemaphoreType.DMA],
        us=25,
    )


def enc_square_grads(meta, n1, n1_got, c, c_got, dq, dk, dv, da, got):
    def body(meta, n1, n1_got, c, c_got, dq, dk, dv, da, got, keep_a, send_a, keep_b, send_b, buf, sems):
        for core, (one, left, left_got, two) in enumerate(((dq, c, c_got, da), (dk, n1, n1_got, dv))):

            @pl.when(meta[1] == core)
            def _():
                buf[0] = (tn(n1[...], one[...]) + tn(n1_got[...], got[0])).astype(BF)
                for g in range(GROUPS):
                    start_store(meta, buf.at[0, pl.ds(g * GROUP, GROUP)], g, 0, keep_a, send_a, sems.at[0])
                buf[1] = (tn(left[...], two[...]) + tn(left_got[...], got[1])).astype(BF)
                for g in range(GROUPS):
                    start_store(meta, buf.at[1, pl.ds(g * GROUP, GROUP)], g, 1, keep_b, send_b, sems.at[1])

        drain(buf.at[0], sems.at[0])
        drain(buf.at[1], sems.at[1])

    return call(
        body, "enc_square_grads", [meta, n1, n1_got, c, c_got, dq, dk, dv, da, got], [SM] + [VM] * 9,
        [(PART, BF)] * 4, [ANY] * 4,
        [pltpu.VMEM((2, D, D), BF), pltpu.SemaphoreType.DMA((2,))],
        us=1,
    )


def enc_input_grad(meta, dq, dk, dv, x, dh1, gains, a_sets, b_sets):
    a_arrays, a_plan = plan_of(a_sets)
    b_arrays, b_plan = plan_of(b_sets)
    n = len(a_arrays)

    def body(meta, dq, dk, dv, x, dh1, gains, *rest):
        a_parts, b_parts, rest = rest[:n], rest[n : 2 * n], rest[2 * n :]
        keep, send, dgain, w, sem = rest
        start_fetch(meta, a_parts, a_plan, [(0, GROUP, lambda core, g: core * D + GROUP * g)], w, sem)
        start_fetch(meta, b_parts, b_plan, [(0, GROUP, lambda core, g: 2 * D + GROUP * g)], w, sem, only=1)
        drain(w, sem)
        total = nt(dq[...], w[0:D, :]) + nt(dk[...], w[D : 2 * D, :]) + nt(dv[...], w[2 * D :, :])
        dx, dg = rms_back(x[...].astype(F32), gains[0:1, :], total)
        out = (dh1[...] + dx).astype(BF)
        dgain[...] = dg
        half = D // 2

        @pl.when(meta[1] == 0)
        def _():
            keep[...] = out[:, :half]
            send[...] = out[:, half:]

        @pl.when(meta[1] != 0)
        def _():
            keep[...] = out[:, half:]
            send[...] = out[:, :half]

    return call(
        body, "enc_input_grad", [meta, dq, dk, dv, x, dh1, gains, *a_arrays, *b_arrays],
        [SM] + [VM] * 6 + [ANY] * (2 * n),
        [((ROW_LEN, D // 2), BF), ((ROW_LEN, D // 2), BF), ((1, D), F32)], [VM] * 3,
        [pltpu.VMEM((3 * D, D), BF), pltpu.SemaphoreType.DMA],
        us=1,
    )


def spread_heads(value):
    return jnp.concatenate([masked(value, head_lanes(h)) for h in range(HEADS)], axis=0)


def join_heads(value):
    total = jnp.zeros((8, D), F32)
    for h in range(HEADS):
        total = total + masked(value[8 * h : 8 * h + 8, :], head_lanes(h))
    return total


def own_rows(meta):
    row = lax.broadcasted_iota(jnp.int32, (8, 1), 0)
    return (row >= 4 * meta[1]) & (row < 4 * meta[1] + 4)


def start_self(meta, own, got, dst, sem):
    half = D // 2
    pltpu.make_async_copy(own, dst.at[pl.ds(pl.multiple_of(meta[1] * half, 16), half)], sem).start()
    pltpu.make_async_copy(got, dst.at[pl.ds(pl.multiple_of((1 - meta[1]) * half, 16), half)], sem).start()


def dec_before(meta, z, d_out, gains, self_own, self_got, sets):
    arrays, plan = plan_of(sets)
    n = len(arrays)

    def body(meta, z, d_out, gains, self_own, self_got, *rest):
        parts, rest = rest[:n], rest[n:]
        m1, sv, z1, m2, qc, qk, gm, w_self, w, sems = rest
        start_self(meta, self_own, self_got, w_self, sems.at[0])
        start_fetch(meta, parts, plan, [(0, GROUP, lambda core, g: core * D + GROUP * g)], w, sems.at[1])
        zf = z[...].astype(F32)
        gm[...] = jnp.where(own_rows(meta), d_out[...].astype(F32), 0.0).astype(BF)
        m1v = rms(zf, gains[2:3, :]).astype(BF)
        drain(w_self, sems.at[0])
        drain(w, sems.at[1])
        svv = nn(m1v, w_self[:, :D]).astype(BF)
        z1v = zf + nn(svv, w_self[:, D:])
        m2v = rms(z1v, gains[0:1, :]).astype(BF)
        qcv = nn(m2v, w[0:D, :]).astype(BF)
        qk[...] = nt(spread_heads(qcv), w[D:, :]).astype(BF)
        m1[...], sv[...], z1[...], m2[...], qc[...] = m1v, svv, z1v, m2v, qcv

    rows = (8, D)
    return call(
        body, "dec_before", [meta, z, d_out, gains, self_own, self_got, *arrays],
        [SM, VM, VM, VM, ANY, ANY] + [ANY] * n,
        [(rows, BF), (rows, BF), (rows, F32), (rows, BF), (rows, BF), ((8 * HEADS, D), BF), (rows, BF)], [VM] * 7,
        [pltpu.VMEM((D, 2 * D), BF), pltpu.VMEM((2 * D, D), BF), pltpu.SemaphoreType.DMA((2,))],
        us=6,
    )


def dec_core(meta, e, segr, qk, qc, z1, g, gw, gains, sets):
    arrays, plan = plan_of(sets)
    n = len(arrays)

    def body(meta, e, segr, qk, qc, z1, g, gw, gains, *rest):
        parts, rest = rest[:n], rest[n:]
        de, cc, z2, m3, fc, duc, da2, dz2, dcc, edt, ebar, dgain, de_other, pairs_other, w, w_in, sems = rest
        start_fetch(meta, parts, plan, [(GROUP, GROUP, lambda core, g: core * D + GROUP * g)], w, sems.at[0])
        start_fetch(meta, parts, plan, in_items(2 * GROUP), w_in, sems.at[pl.ds(1, 4)])
        pairs = lax.broadcasted_iota(jnp.int32, (8 * HEADS, 1), 0)
        owner = segr[...] == jnp.bitwise_and(pairs, 7) - 4 * meta[1]
        t = jnp.where(owner, nt(qk[...], e[...]), MASKED)
        ex = jnp.where(owner, jnp.exp(t - jnp.max(t, axis=-1, keepdims=True)), 0.0)
        tot = jnp.sum(ex, axis=-1, keepdims=True)
        prob = ex * (1.0 / jnp.where(tot > 0.0, tot, 1.0))
        pc = prob.astype(BF)
        ebv = nn(pc, e[...]).astype(BF)
        ebar[...] = ebv
        drain(w, sems.at[0])
        ccv = join_heads(nn(ebv, w[D:, :])).astype(BF)
        z2v = z1[...] + nn(ccv, w[0:D, :])
        m3v = rms(z2v, gains[1:2, :]).astype(BF)
        dm3 = jnp.zeros((8, D), F32)
        own = own_rows(meta)
        for b in (0, 2, 1, 3):
            cols = slice(b * D, (b + 1) * D)
            drain(w_in.at[cols], sems.at[1 + b])
            value, slope = gelu_both(nn(m3v, w_in[cols, :]))
            fc[:, cols] = jnp.where(own, value, 0.0).astype(BF)
            ducv = jnp.where(own, slope * gw[:, cols].astype(F32), 0.0).astype(BF)
            duc[:, cols] = ducv
            dm3 = dm3 + nt(ducv, w_in[cols, :])
        back, dg = rms_back(z2v, gains[1:2, :], dm3)
        dz2v = g[...].astype(F32) + back
        da2v = dz2v.astype(BF)
        dccv = nt(da2v, w[0:D, :]).astype(BF)
        dvw = nt(spread_heads(dccv), w[D:, :]).astype(BF)
        dprob = nt(dvw, e[...])
        dt = (prob * (dprob - jnp.sum(prob * dprob, axis=-1, keepdims=True))).astype(BF)
        de[...] = tn(jnp.concatenate([pc, dt], axis=0), jnp.concatenate([dvw, qk[...]], axis=0)).astype(BF)
        edt[...] = nn(dt, e[...]).astype(BF)
        cc[...], m3[...], da2[...], dz2[...], dcc[...], dgain[...] = ccv, m3v, da2v, dz2v, dccv, dg
        z2[...] = jnp.where(own, z2v, 0.0)
        half = D // 2
        pairs_other[8 * HEADS + 8 :, :] = jnp.zeros((8, D), BF)

        @pl.when(meta[1] == 0)
        def _():
            de_other[...] = de[:, half:]
            pairs_other[: 8 * HEADS, :] = ebv
            pairs_other[8 * HEADS : 8 * HEADS + 8, :] = dccv

        @pl.when(meta[1] != 0)
        def _():
            de_other[...] = de[:, :half]
            pairs_other[: 8 * HEADS, :] = edt[...]
            pairs_other[8 * HEADS : 8 * HEADS + 8, :] = qc[...]

    rows, spread = (8, D), (8 * HEADS, D)
    return call(
        body, "dec_core", [meta, e, segr, qk, qc, z1, g, gw, gains, *arrays],
        [SM] + [VM] * 8 + [ANY] * n,
        [((ROW_LEN, D), BF), (rows, BF), (rows, F32), (rows, BF), ((8, FF), BF), ((8, FF), BF), (rows, BF),
         (rows, F32), (rows, BF), (spread, BF), (spread, BF), ((1, D), F32),
         ((ROW_LEN, D // 2), BF), ((8 * HEADS + 16, D), BF)], [VM] * 14,
        [pltpu.VMEM((2 * D, D), BF), pltpu.VMEM((FF, D), BF), pltpu.SemaphoreType.DMA((5,))],
        us=10,
    )


def dec_after(meta, z, z1, dz2, qc, dcc, edt, ebar, got, gains, acts, duc, fc, self_own, self_got, sets):
    arrays, plan = plan_of(sets)
    n = len(arrays)

    def body(meta, z, z1, dz2, qc, dcc, edt, ebar, got, gains, *rest):
        acts, rest = rest[:8], rest[8:]
        self_own, self_got, parts, rest = rest[0], rest[1], rest[2 : 2 + n], rest[2 + n :]
        acts_keep, acts_send, dec_grad, dg_attn, dg_self, keep, send, w_self, w, buf, sems = rest
        start_fetch(meta, parts, plan, [(0, GROUP, lambda core, g: core * D + GROUP * g)], w, sems.at[1])
        start_self(meta, self_own, self_got, w_self, sems.at[0])
        zero = meta[1] == 0
        left = jnp.concatenate([jnp.where(zero, edt[...], ebar[...]), got[: 8 * HEADS, :]], axis=0)
        right = jnp.where(zero, qc[...], dcc[...])
        right = jnp.concatenate([spread_heads(right), spread_heads(got[8 * HEADS : 8 * HEADS + 8, :])], axis=0)
        buf[...] = tn(left, right).astype(BF)
        for grp in range(GROUPS):
            start_store(meta, buf.at[pl.ds(grp * GROUP, GROUP)], grp, 0, keep, send, sems.at[3], pl.ds(GROUP, GROUP))
        drain(w, sems.at[1])
        dqv = join_heads(nn(edt[...], w[D:, :])).astype(BF)
        back, dg = rms_back(z1[...], gains[0:1, :], nt(dqv, w[0:D, :]))
        dz1 = dz2[...] + back
        ds1v = dz1.astype(BF)
        drain(w_self, sems.at[0])
        dsvv = nt(ds1v, w_self[:, D:]).astype(BF)
        back0, dg0 = rms_back(z[...].astype(F32), gains[2:3, :], nt(dsvv, w_self[:, :D]))
        own = own_rows(meta)
        dec_grad[...] = jnp.where(own, dz1 + back0, 0.0).astype(BF)
        dg_attn[...], dg_self[...] = dg, dg0
        row = jnp.concatenate([ref[...] for ref in acts[:6]] + [dqv, ds1v, dsvv] + [ref[...] for ref in acts[6:]], axis=1)
        half = row.shape[1] // 2
        for core, (one, two) in enumerate(((acts_keep, acts_send), (acts_send, acts_keep))):

            @pl.when(meta[1] == core)
            def _():
                one[...] = row[:, :half]
                two[...] = row[:, half:]

        drain(buf, sems.at[3])

    rows = (8, D)
    return call(
        body, "dec_after",
        [meta, z, z1, dz2, qc, dcc, edt, ebar, got, gains, *acts, duc, fc, self_own, self_got, *arrays],
        [SM] + [VM] * 17 + [ANY] * (2 + n),
        [((8, (9 * D + 2 * FF) // 2), BF)] * 2 + [(rows, BF)] + [((1, D), F32)] * 2 + [(WIDE_PART, BF)] * 2, [VM] * 5 + [ANY] * 2,
        [pltpu.VMEM((D, 2 * D), BF), pltpu.VMEM((2 * D, D), BF), pltpu.VMEM((D, D), BF),
         pltpu.SemaphoreType.DMA((4,))],
        us=6,
    )


def dec_weight_grads(place, own, got, g_all, w_back, rows, self_rows):
    def body(place, own, got, *rest):
        for core, (left, right) in enumerate(((own, got), (got, own))):
            pl.when(place[1] == core)(functools.partial(halves, place, left, right, *rest))

    def halves(place, left, right, g_all, w_back, dec_q, dec_o, dec_i, dec_b, self_v, self_o, y):
        half = left.shape[1]
        chip, core = place[0], place[1]
        chips = D // rows

        def cut(at, width):
            parts = []
            while width:
                ref, first = (left, at) if at < half else (right, at - half)
                count = min(width, half - first)
                parts.append(ref[:, first : first + count])
                at, width = at + count, width - count
            return parts[0] if len(parts) == 1 else jnp.concatenate(parts, axis=1)

        def picked(at, first, count, width=D):
            row = lax.broadcasted_iota(jnp.int32, (count, width), 0) + first
            col = lax.broadcasted_iota(jnp.int32, (count, width), 1)
            return nt((row == col).astype(F32).astype(BF), cut(at * D, width)).astype(BF)

        first, first_self = chip * rows, (core * chips + chip) * self_rows
        m1, sv, m2, cc, m3, da2, dqc, ds1, dsv, duc, fc = list(range(10)) + [13]
        dec_q[...] = nn(picked(m2, first, rows), cut(dqc * D, D))
        dec_o[...] = nn(picked(cc, first, rows), cut(da2 * D, D))
        dec_i[...] = nn(picked(m3, first, rows), cut(duc * D, FF))
        self_v[...] = nn(picked(m1, first_self, self_rows), cut(dsv * D, D))
        self_o[...] = nn(picked(sv, first_self, self_rows), cut(ds1 * D, D))
        hidden = picked(fc, 4 * first, 4 * rows, FF)
        dec_b[...] = nn(hidden, g_all[...])
        y[...] = tn(hidden, w_back[...]).astype(BF)

    return call(
        body, "dec_weight_grads", [place, own, got, g_all, w_back], [SM, VM, VM, VM, VM],
        [((rows, D), F32), ((rows, D), F32), ((rows, FF), F32), ((4 * rows, D), F32), ((self_rows, D), F32),
         ((self_rows, D), F32), (g_all.shape, BF)], [VM] * 7,
        [], us=5,
    )


def prepare(meta, w_query, w_key, w_value, w_out, w_in, w_back):
    def body(meta, query, key, value, out, w_in, w_back, kept, sent):
        for core, (one, two) in enumerate(((kept, sent), (sent, kept))):

            @pl.when(meta[1] == core)
            def _():
                for half, (dst, squares) in enumerate(((one, (query, out)), (two, (key, value)))):
                    for k in range(2):
                        at = 2 * half + k
                        dst[k * GROUP : (k + 1) * GROUP, :] = squares[k][...]
                        dst[(2 + k) * GROUP : (3 + k) * GROUP, :] = w_in[:, at * D : (at + 1) * D]
                        dst[(4 + k) * GROUP : (5 + k) * GROUP, :] = w_back[at * GROUP : (at + 1) * GROUP, :]

    half = ((6 * GROUP, D), BF)
    return call(
        body, "prepare", [meta, w_query, w_key, w_value, w_out, w_in, w_back], [SM] + [VM] * 6, [half] * 2, [VM] * 2, [], us=2
    )


def per_device(
    enc_in, dec_in, segment, d_out, attn_gain, w_query, w_key, w_value, w_out, ffn_gain, w_in, w_back,
    self_gain, self_value, self_out, rel_table,
):
    core, chip = lax.axis_index("section"), lax.axis_index("dp")
    chips = lax.axis_size("dp")
    rows = w_query.shape[1]
    first = core == 0
    pre = low_bits(rows)
    meta = jnp.stack([chip >> pre, core]).astype(jnp.int32)
    self_rows = self_value.shape[0]
    at_self = (core * chips + chip) * self_rows

    kept, sent = prepare(
        meta, *[filled(w[0], pre, chip, 0) for w in (w_query, w_key, w_value, w_out, w_in, w_back)]
    )
    got = across(sent)
    enc_piece, dec_piece = jnp.where(first, kept, got), jnp.where(first, got, kept)
    count = 4 * GROUP

    shared = lax.all_gather(jnp.concatenate([dec_piece[:count], self_value, self_out, enc_piece[5 * GROUP :]]), "dp")

    gains = jnp.zeros((8, D), BF)
    gains = lax.dynamic_update_slice(gains, jnp.concatenate([attn_gain, ffn_gain]), (0, chip * rows))
    gains = lax.dynamic_update_slice(gains, self_gain[None], (2, at_self))
    little = Chain([jnp.concatenate([gains, d_out])[None]], [0], 0)
    for bit in range(pre):
        little.step(bit)

    def chain(*parts):
        return Chain([jnp.concatenate(parts)[None]], [0], pre)

    cut = 3 * GROUP + 2 * GROUP // 3
    sq = chain(enc_piece[: 2 * GROUP])
    wide = chain(enc_piece[2 * GROUP : cut], enc_piece[4 * GROUP : 5 * GROUP], enc_piece[cut : 4 * GROUP])

    windows = jnp.einsum(
        "adtb,bh->hadt", window_onehots(), rel_table, precision=lax.Precision.HIGHEST
    ).reshape(HEADS, 6, 2 * TILE)
    x = lax.dynamic_index_in_dim(enc_in, core, 0, False)
    seg = lax.dynamic_index_in_dim(segment, core, 0, False)
    segr, segc = seg[None, :], seg[:, None]

    sq.step(Z1), little.step(X + pre)
    phase(sq, little)
    sq.step(Z0), little.step(Y + pre)
    phase(sq, wide, little)
    sa, sb = sq.split(GROUP)
    sa.step(X), sb.step(Y), wide.step(Z1), little.step(Z0 + pre)
    phase(sa, sb, wide, little)
    sa.step(Y), sb.step(X), wide.step(Z0), little.step(Z1 + pre)
    sa_got, sb_got = [across(sa.parts[0])], [across(sb.parts[0])]
    x = phase(sa, sb, wide, little, x)
    wa, wb = wide.split(cut - 2 * GROUP)
    wa.step(X), wb.step(Y)
    sa_got += [across(sa.parts[1])]
    sb_got += [across(sb.parts[1])]

    order = np.argsort(np.array(little.ids))
    places = jnp.take(jnp.asarray(order, jnp.int32), jnp.bitwise_xor(jnp.arange(chips), chip))
    little = jnp.concatenate(little.parts)
    gains = jnp.sum(little[:, :8].astype(F32), axis=0)
    gains_got = across(gains)
    gains0, gains1 = jnp.where(first, gains, gains_got), jnp.where(first, gains_got, gains)
    gains1 = jnp.where(jnp.arange(8)[:, None] == 2, gains0 + gains1, gains1)
    n1, q, k, v, c, h1, n2, lse = enc_attention(meta, x, gains0, segr, segc, windows, sa.sets(sa_got), sb.sets(sb_got))
    h1, little = phase(wa, wb, h1, little)
    wa.step(Y), wb.step(X)
    wa_got, wb_got = [across(wa.parts[0])], [across(wb.parts[0])]

    g_all = jnp.take(little[:, 8:], places, axis=0).reshape(8 * chips, D)
    lanes = -(-4 * rows // TILE) * TILE
    gw = jnp.pad(nt(g_all, w_back[0]).astype(BF), ((0, 0), (0, lanes - 4 * rows))).reshape(chips, 8, lanes)
    gw = lax.all_to_all(gw, "dp", 0, 0)
    h1, shared, gw = phase(wa, wb, h1, shared, gw)
    wa_got += [across(wa.parts[1])]
    wb_got += [across(wb.parts[1])]
    back_at = count + 2 * self_rows
    shared_back = shared[:: 2**pre, back_at:]
    back_got = across(shared_back)

    def self_part(index):
        at = count + index * self_rows
        return shared[:, at : at + self_rows].reshape(D // 2, D)

    self_own = jnp.concatenate([self_part(0), self_part(1)], axis=1)
    gw = gw[:, :, : 4 * rows].transpose(1, 0, 2).reshape(8, FF)
    gw_got = across(gw)
    wa_got, wb_got, back_got, h1, n1, c, n2, shared, self_own, gw, gw_got = phase(
        wa_got, wb_got, back_got, h1, n1, c, n2, shared, self_own, gw, gw_got
    )
    gw = jnp.where(first, gw_got, gw)
    self_got, shared_got = across(self_own), across(shared)
    n1_got, c_got, n2_got = across(n1), across(c), across(n2)
    w_in_from = in_sources(wa.sets(wa_got), wb.sets(wb_got))
    w_back_from = back_sources(wb.sets(wb_got), shared_back if pre else shared, 0 if pre else back_at, back_got)
    f, slope, e = enc_ffn(meta, h1, n2, w_in_from, w_back_from)
    e, shared_got, n1_got, c_got, n2_got, self_got = phase(e, shared_got, n1_got, c_got, n2_got, self_got)
    dec_sets = [(v[:: 2**pre] if pre else v, None, other) for other, v in enumerate((shared, shared_got))]
    m1, sv, z1, m2, qc, qk, gm = dec_before(meta, dec_in, d_out, gains1, self_own, self_got, dec_sets)
    f, qk = phase(f, qk)
    f_got = across(f)
    de, cc, z2, m3, fc, duc, da2, dz2, dcc, edt, ebar, dg_ffn1, de_other, pairs_other = dec_core(
        meta, e, segr, qk, qc, z1, gm, gw, gains1, dec_sets
    )

    def two(parts):
        return Sum(parts[0], parts[1], pre), Sum(parts[2], parts[3], pre)

    de_got, pairs_got = across(de_other), across(pairs_other)
    du, du_other = enc_hidden_grad(meta, de, slope, w_back_from)
    de_got, pairs_got, du, du_other, edt = phase(de_got, pairs_got, du, du_other, edt)
    du_got = across(du_other)
    acts, acts_send, dec_grad, dg_attn1, dg_self, k_keep, k_send = dec_after(
        meta, dec_in, z1, dz2, qc, dcc, edt, ebar, pairs_got, gains1, [m1, sv, m2, cc, m3, da2], duc, fc,
        self_own, self_got, dec_sets,
    )
    acts, acts_send, f, f_got = phase(acts, acts_send, f, f_got)
    acts_got, width = across(acts_send), acts.shape[1]
    own = (jnp.arange(8)[:, None] // 4) == core
    acts = jnp.where(own, acts, acts_got)
    acts = lax.all_gather(acts, "dp").reshape(8 * chips, width)
    back_a, back_b = two(enc_w_back_grad(meta, de, de_got, f, f_got))
    n2, du_got = phase(back_a, back_b, n2, du_got)
    back_a.step(Y), back_b.step(X)
    in_a, in_b = two(enc_w_in_grad(meta, du, du_got, n2, n2_got, k_keep, k_send))
    h1 = phase(in_a, in_b, h1)
    in_a.step(Y), in_b.step(X)
    dh1, da, dg_ffn0 = enc_ffn_back(meta, du, h1, de, gains0, w_in_from)
    da = phase(back_a, back_b, da)
    back_a.step(X), back_b.step(Y)
    dq, dk, dv, diag, other = enc_attention_back(meta, da, q, k, v, lse, segr, segc, windows, sb.sets(sb_got))
    dq, other = phase(back_a, back_b, in_a, in_b, dq, other)
    got = across(other)
    in_a.step(X), in_b.step(Y)
    backs = merged([back_a, back_b])
    backs.step(Z0)
    keep, send, dg_attn0 = enc_input_grad(meta, dq, dk, dv, x, dh1, gains0, sa.sets(sa_got), sb.sets(sb_got))
    got, dq, dg_attn0 = phase(backs, got, dq, dg_attn0)
    backs.step(Z1)
    square_a, square_b = two(enc_square_grads(meta, n1, n1_got, c, c_got, dq, dk, dv, da, got))
    table = jnp.einsum("hdt,dtb->bh", diag, diagonal_onehots(), precision=lax.Precision.HIGHEST)
    little = jnp.concatenate([
        dg_attn0, dg_ffn0, dg_attn1, dg_ffn1, dg_self,
        jnp.pad(table.reshape(1, -1), ((0, 0), (0, D - BUCKETS * HEADS))), jnp.zeros((2, D), F32),
    ])
    little = little + across(little)
    for bit in range(pre):
        little = little + along(little, bit)
    acts, little = phase(square_a, square_b, in_a, in_b, acts, little)
    square_a.step(Y), square_b.step(X)
    theirs = across(acts)
    other = along(little, X + pre)
    ins = merged([in_a, in_b])
    ins.step(Z0)

    dec_q, dec_o, dec_i, dec_b, g_self_value, g_self_out, y = dec_weight_grads(
        jnp.stack([chip, core]), acts, theirs, g_all, w_back[0], rows, self_rows
    )
    other, y = phase(square_a, square_b, ins, backs, other, y)
    little = little + other
    square_a.step(X), square_b.step(Y), ins.step(Z1)
    other = along(little, Y + pre)
    other, y, send, z2 = phase(square_a, square_b, other, y, send, z2)
    little = little + other
    squares = merged([square_a, square_b])
    squares.step(Z0)
    other = along(little, Z0 + pre)
    z2 = z2 + across(z2)
    y = lax.all_to_all(y.reshape(chips, 8, D), "dp", 0, 0)
    other, y = phase(squares, ins, other, y)
    little = little + other
    squares.step(Z1)
    little = little + along(little, Z1 + pre)
    backs_sum, ins_sum, square_sum = backs.total(), ins.total(), squares.total()
    dec_out = (z2 + jnp.sum(y.astype(F32), axis=0)).astype(BF)
    dec_out = jnp.where(first, across(dec_out), dec_out)
    mine = chip * rows

    g_rel_table = little[5, : BUCKETS * HEADS].reshape(BUCKETS, HEADS)

    def cut(index, at, count):
        return lax.dynamic_slice_in_dim(little[index], at, count, 0)

    g_attn_gain = cut(jnp.where(first, 0, 2), mine, rows)[None]
    g_ffn_gain = cut(jnp.where(first, 1, 3), mine, rows)[None]
    g_self_gain = cut(4, at_self, self_rows)

    backs_got, ins_got, square_got = [across(v.astype(BF)).astype(F32) for v in (backs_sum, ins_sum, square_sum)]

    def group(value, index):
        return value[index * GROUP : (index + 1) * GROUP]

    def placed(enc_value, dec_value):
        return jnp.where(first, narrowed(enc_value, pre, chip), dec_value)[None]

    g_w_query = placed(group(square_sum, 0), dec_q)
    g_w_out = placed(group(square_sum, 1), dec_o)
    g_w_key = narrowed(jnp.where(first, group(square_got, 0), group(ins_got, 1)), pre, chip)[None]
    g_w_value = narrowed(jnp.where(first, group(square_got, 1), group(ins_sum, 1)), pre, chip)[None]
    g_w_in = placed(
        jnp.concatenate([group(ins_sum, 0), group(ins_sum, 2), group(ins_got, 0), group(ins_got, 2)], axis=1), dec_i
    )
    half = D // 2
    tall = [
        jnp.concatenate([group(v, i)[:, j * half : (j + 1) * half] for i in range(2) for j in range(2)])
        for v in (backs_sum, backs_got)
    ]
    g_w_back = placed(jnp.concatenate(tall, axis=1), dec_b)

    other_half = across(send)
    enc_in_grad = jnp.where(first, jnp.stack([keep, other_half]), jnp.stack([other_half, keep]))
    dec_grad = dec_grad + across(dec_grad)
    half = D // 2
    dec_out = jnp.where(first, dec_out[:, :half], dec_out[:, half:])
    dec_in_grad = jnp.where(first, dec_grad[:, :half], dec_grad[:, half:])
    return (
        dec_out, enc_in_grad, dec_in_grad, g_attn_gain, g_w_query, g_w_key, g_w_value, g_w_out, g_ffn_gain,
        g_w_in, g_w_back, g_self_gain, g_self_value, g_self_out, g_rel_table,
    )


def solution(mesh):
    return jax.shard_map(
        per_device,
        mesh=mesh,
        in_specs=(
            P("dp", None, None),
            P("dp", None),
            P("dp", None),
            P("dp", None),
            P("section", "dp"),
            P("section", "dp", None),
            P("section", "dp", None),
            P("section", "dp", None),
            P("section", "dp", None),
            P("section", "dp"),
            P("section", "dp", None),
            P("section", "dp", None),
            P(("section", "dp")),
            P(("section", "dp"), None),
            P(("section", "dp"), None),
            P(),
        ),
        out_specs=(
            P("dp", "section"),
            P("dp", None, "section"),
            P("dp", "section"),
            P("section", "dp"),
            P("section", "dp", None),
            P("section", "dp", None),
            P("section", "dp", None),
            P("section", "dp", None),
            P("section", "dp"),
            P("section", "dp", None),
            P("section", "dp", None),
            P(("section", "dp")),
            P(("section", "dp"), None),
            P(("section", "dp"), None),
            P(),
        ),
        check_vma=False,
    )
```

profile of v0, /device:TPU:0, one launch (start us, length us, event | category | flops | bytes accessed | tf_op | source)
XLA Modules:
  0.0 369.7 jit_solution(4641536958262538352)
XLA Ops:
  7.8 2.2 prepare.1
  10.6 1.6 collective-permute-done
  14.9 3.3 collective-permute-start.2
  19.4 2.7 collective-permute-start.1
  24.9 3.2 collective-permute-done.1
  28.2 3.3 collective-permute-start.3
  32.2 3.4 collective-permute-done.4
  35.6 8.9 %collective-permute-done.3 = bf16[2,96,768]{2,1,0:T(8,128)(2,1)S(1)} collective-permute-done((bf16[2,96,768]{2,1,0:T(8,128)(2,1)S(1)}, bf16[2,96,768]{2,1,0:T(8,128)(2,1)S(1)}, u32[]{:S(2)}, u32[]{:S(2)}) %collective-permute-start.3) | collective-permute-done | bytes 294944 | tf_op jit(solution)/shard_map/ppermute | solution.py:68
  46.9 1.8 collective-permute-start.7
  48.7 1.8 collective-permute-start.8
  50.5 9.8 %collective-permute-done.8 = bf16[4,16,768]{2,1,0:T(8,128)(2,1)S(1)} collective-permute-done((bf16[4,16,768]{2,1,0:T(8,128)(2,1)S(1)}, bf16[4,16,768]{2,1,0:T(8,128)(2,1)S(1)}, u32[]{:S(2)}, u32[]{:S(2)}) %collective-permute-start.8) | collective-permute-done | bytes 98336 | tf_op jit(solution)/shard_map/ppermute | solution.py:68
  60.3 9.7 %collective-permute-done.7 = bf16[1,144,768]{2,1,0:T(8,128)(2,1)S(1)} collective-permute-done((bf16[1,144,768]{2,1,0:T(8,128)(2,1)S(1)}, bf16[1,144,768]{2,1,0:T(8,128)(2,1)S(1)}, u32[]{:S(2)}, u32[]{:S(2)}) %collective-permute-start.7) | collective-permute-done | bytes 221216 | tf_op jit(solution)/shard_map/ppermute | solution.py:68
  71.4 3.3 collective-permute-start.12
  74.7 13.7 %collective-permute-done.12 = bf16[8,16,768]{2,1,0:T(8,128)(2,1)S(1)} collective-permute-done((bf16[8,16,768]{2,1,0:T(8,128)(2,1)S(1)}, bf16[8,16,768]{2,1,0:T(8,128)(2,1)S(1)}, u32[]{:S(2)}, u32[]{:S(2)}) %collective-permute-start.12) | collective-permute-done | bytes 196640 | tf_op jit(solution)/shard_map/ppermute | solution.py:68
  88.4 2.3 collective-permute-done.11
  91.8 2.0 collective-permute-done.15
  97.8 20.3 %enc_attention.1 = (bf16[512,768]{1,0:T(8,128)(2,1)}, bf16[512,768]{1,0:T(8,128)(2,1)}, bf16[512,768]{1,0:T(8,128)(2,1)}, bf16[512,768]{1,0:T(8,128)(2,1)}, bf16...) custom-call(s32[2]{0:T(128)} %pad_add_fusion.meta, ...), custom_call_target="tpu_custom_call" | custom-call | flops 5500000256 | bytes 5000000 | tf_op jit(solution)/shard_map/enc_attention/pallas_call | solution.py:347
  118.1 1.8 collective-permute-done.13
  123.4 1.7 collective-permute-start.22
  126.2 20.5 %all_to_all.10 = bf16[16,8,256]{2,1,0:T(8,128)(2,1)S(1)} all-to-all(bf16[16,8,256]{2,1,0:T(8,128)(2,1)S(1)} %pad_bitcast_fusion), channel_id=1, replica_groups=mesh['section'=2,'dp'=16] {'dp'}, dimensions={0} | all-to-all | bytes 131072 | tf_op jit(solution)/shard_map/all_to_all | solution.py:1032
  146.8 2.6 slice.323
  151.9 2.2 collective-permute-done.24.rest_6_.rest_10_.rest_2_
  154.6 1.6 collective-permute-done.20.rest_2_
  158.9 15.8 %enc_ffn.1 = (bf16[512,3072]{1,0:T(8,128)(2,1)}, bf16[512,3072]{1,0:T(8,128)(2,1)}, bf16[512,768]{1,0:T(8,128)(2,1)}) custom-call(s32[2]{0:T(128)} %pad_add_fusion.meta, f32[512,768]{1,0:T(8,128)} %get-tuple-element.337.h1, bf16[512,768]{1,0:T(8,128)(2,1)} %get-tuple-element.329.n2, bf16[8,80,768]{2,1,0:T(8,128)(2,1)} %constant_dynamic-update-slice_fusion.16.rest_0_, ...), custom_call_target="tpu_custom_call" | custom-call | flops 4124999936 | bytes 3750000 | tf_op jit(solution)/shard_map/enc_ffn/pallas_call | solution.py:347
  175.9 5.1 %dec_before.1 = (bf16[8,768]{1,0:T(8,128)(2,1)}, bf16[8,768]{1,0:T(8,128)(2,1)}, f32[8,768]{1,0:T(8,128)}, bf16[8,768]{1,0:T(8,128)(2,1)}, bf16[8,768]{1,0:T(8,1...) custom-call(s32[2]{0:T(128)} %pad_add_fusion.meta, bf16[8,768]{1,0:T(8,128)(2,1)} %z.3, bf16[8,768]{1,0:T(8,128)(2,1)} %d_out.1, ...), custom_call_target="tpu_custom_call" | custom-call | flops 1650000000 | bytes 1500000 | tf_op jit(solution)/shard_map/dec_before/pallas_call | solution.py:347
  182.1 9.6 %dec_core.1 = (bf16[512,768]{1,0:T(8,128)(2,1)}, bf16[8,768]{1,0:T(8,128)(2,1)}, f32[8,768]{1,0:T(8,128)}, bf16[8,768]{1,0:T(8,128)(2,1)}, bf16[8,3072]{1,0:T(8,...) custom-call(s32[2]{0:T(128)} %pad_add_fusion.meta, ...), custom_call_target="tpu_custom_call" | custom-call | flops 2750000128 | bytes 2500000 | tf_op jit(solution)/shard_map/dec_core/pallas_call | solution.py:347
  192.3 9.6 %enc_hidden_grad.1 = (bf16[512,3072]{1,0:T(8,128)(2,1)}, bf16[512,1536]{1,0:T(8,128)(2,1)}) custom-call(s32[2]{0:T(128)} %pad_add_fusion.meta, bf16[512,768]{1,0:T(8,128)(2,1)} %get-tuple-element.292.de, bf16[512,3072]{1,0:T(8,128)(2,1)} %get-tuple-element.295.slope, bf16[8,64,768]{2,1,0:T(8,128)(2,1)} %copy-done.2, bf16[8,64,768]{2,1,0:T(8,128)(2,1)} %copy-done.3, ...), custom_call_target="tpu_custom_call" | custom-call | flops 2200000000 | bytes 2000000 | tf_op jit(solution)/shard_map/enc_hidden_grad/pallas_call | solution.py:347
  202.7 6.0 %dec_after.1 = (bf16[8,6528]{1,0:T(8,128)(2,1)}, bf16[8,6528]{1,0:T(8,128)(2,1)}, bf16[8,768]{1,0:T(8,128)(2,1)}, f32[1,768]{1,0:T(1,128)}, f32[1,768]{1,0:T(1,1...) custom-call(s32[2]{0:T(128)} %pad_add_fusion.meta, bf16[8,768]{1,0:T(8,128)(2,1)} %z.3, ...), custom_call_target="tpu_custom_call" | custom-call | flops 1650000000 | bytes 1500000 | tf_op jit(solution)/shard_map/dec_after/pallas_call | solution.py:347
  210.4 8.1 %enc_w_back_grad.1 = (bf16[8,48,768]{2,1,0:T(8,128)(2,1)}, bf16[8,48,768]{2,1,0:T(8,128)(2,1)}, bf16[8,48,768]{2,1,0:T(8,128)(2,1)}, bf16[8,48,768]{2,1,0:T(8,128)(2,1)}) custom-call(s32[2]{0:T(128)} %pad_add_fusion.meta, bf16[512,768]{1,0:T(8,128)(2,1)} %get-tuple-element.292.de, bf16[512,384]{1,0:T(8,128)(2,1)} %copy-done.30, ...), custom_call_target="tpu_custom_call" | custom-call | flops 1924999936 | bytes 1750000 | tf_op jit(solution)/shard_map/enc_w_back_grad/pallas_call | solution.py:347
  221.3 6.6 %enc_w_in_grad.1 = (bf16[8,96,768]{2,1,0:T(8,128)(2,1)}, bf16[8,96,768]{2,1,0:T(8,128)(2,1)}, bf16[8,48,768]{2,1,0:T(8,128)(2,1)}, bf16[8,48,768]{2,1,0:T(8,128)(2,1)}) custom-call(s32[2]{0:T(128)} %pad_add_fusion.meta, bf16[512,3072]{1,0:T(8,128)(2,1)} %get-tuple-element.327.du, ...), custom_call_target="tpu_custom_call", output_to_operand_aliasing={{0}: (5, {}), {1}: (6, {})} | custom-call | flops 1924999936 | bytes 1750000 | tf_op jit(solution)/shard_map/enc_w_in_grad/pallas_call | solution.py:347
  229.5 10.1 %enc_ffn_back.1 = (f32[512,768]{1,0:T(8,128)}, bf16[512,768]{1,0:T(8,128)(2,1)}, f32[1,768]{1,0:T(1,128)}) custom-call(s32[2]{0:T(128)} %pad_add_fusion.meta, bf16[512,3072]{1,0:T(8,128)(2,1)} %get-tuple-element.327.du, f32[512,768]{1,0:T(8,128)} %get-tuple-element.337.h1, bf16[512,768]{1,0:T(8,128)(2,1)} %get-tuple-element.292.de, ...), custom_call_target="tpu_custom_call" | custom-call | flops 2200000000 | bytes 2000000 | tf_op jit(solution)/shard_map/enc_ffn_back/pallas_call | solution.py:347
  242.7 23.9 %enc_attention_back.1 = (bf16[512,768]{1,0:T(8,128)(2,1)}, bf16[512,768]{1,0:T(8,128)(2,1)}, bf16[512,768]{1,0:T(8,128)(2,1)}, f32[12,5,256]{2,1,0:T(8,128)}, bf16[2,512,768]{2,1,0:T(8,128)(2,1)}) custom-call(s32[2]{0:T(128)} %pad_add_fusion.meta, bf16[512,768]{1,0:T(8,128)(2,1)} %get-tuple-element.347.da, bf16[512,768]{1,0:T(8,128)(2,1)} %get-tuple-element.348.q, ...), custom_call_target="tpu_custom_call" | custom-call | flops 6874999808 | bytes 6250000 | tf_op jit(solution)/shard_map/enc_attention_back/pallas_call | solution.py:347
  266.6 1.7 collective-permute-done.40
  274.4 8.0 %enc_input_grad.1 = (bf16[512,384]{1,0:T(8,128)(2,1)}, bf16[512,384]{1,0:T(8,128)(2,1)}, f32[1,768]{1,0:T(1,128)}) custom-call(s32[2]{0:T(128)} %pad_add_fusion.meta, bf16[512,768]{1,0:T(8,128)(2,1)} %get-tuple-element.364.dq, bf16[512,768]{1,0:T(8,128)(2,1)} %get-tuple-element.360.dk, bf16[512,768]{1,0:T(8,128)(2,1)} %get-tuple-element.361.dv, ...), custom_call_target="tpu_custom_call" | custom-call | flops 275000000 | bytes 250000 | tf_op jit(solution)/shard_map/enc_input_grad/pallas_call | solution.py:347
  282.4 3.0 collective-permute-done.43
  286.3 7.1 %enc_square_grads.1 = (bf16[8,48,768]{2,1,0:T(8,128)(2,1)}, bf16[8,48,768]{2,1,0:T(8,128)(2,1)}, bf16[8,48,768]{2,1,0:T(8,128)(2,1)}, bf16[8,48,768]{2,1,0:T(8,128)(2,1)}) custom-call(s32[2]{0:T(128)} %pad_add_fusion.meta, bf16[512,768]{1,0:T(8,128)(2,1)} %get-tuple-element.265.n1, bf16[512,768]{1,0:T(8,128)(2,1)} %copy-done.15, ...), custom_call_target="tpu_custom_call" | custom-call | flops 275000000 | bytes 250000 | tf_op jit(solution)/shard_map/enc_square_grads/pallas_call | solution.py:347
  295.8 1.6 collective-permute-done.64
  301.9 2.2 collective-permute-start.52
  305.9 5.5 %dec_weight_grads.1 = (f32[48,768]{1,0:T(8,128)}, f32[48,768]{1,0:T(8,128)}, f32[48,3072]{1,0:T(8,128)}, f32[192,768]{1,0:T(8,128)}, f32[24,768]{1,0:T(8,128)}, ...) custom-call(s32[2]{0:T(128)} %pad_add_fusion.1.place, bf16[128,6528]{1,0:T(8,128)(2,1)} %all-gather.7.cloned.1.call-done.own, ...), custom_call_target="tpu_custom_call" | custom-call | flops 1375000064 | bytes 1250000 | tf_op jit(solution)/shard_map/dec_weight_grads/pallas_call | solution.py:347
  312.8 3.5 collective-permute-done.53
  321.1 1.9 collective-permute-start.60
  323.0 3.8 %collective-permute-done.56 = bf16[4,48,768]{2,1,0:T(8,128)(2,1)S(1)} collective-permute-done((bf16[4,48,768]{2,1,0:T(8,128)(2,1)S(1)}, bf16[4,48,768]{2,1,0:T(8,128)(2,1)S(1)}, u32[]{:S(2)}, u32[]{:S(2)}) %collective-permute-start.56) | collective-permute-done | bytes 294944 | tf_op jit(solution)/shard_map/ppermute | solution.py:68
  328.1 1.7 collective-permute-start.59
  329.8 4.4 %all-to-all-start.1 = ((bf16[16,8,768]{2,1,0:T(8,128)(2,1)}), bf16[16,8,768]{2,1,0:T(8,128)(2,1)S(1)}, u32[]{:S(2)}, u32[]{:S(2)}) async-start(bf16[16,8,768]{2,1,0:T(8,128)(2,1)} %bitcast.31), calls=%async_computation.1 | async-start | bytes 393216 | tf_op jit(solution)/shard_map/all_to_all | solution.py:1128
  334.3 2.0 collective-permute-start.61
  337.7 5.7 %collective-permute-done.61 = f32[8,768]{1,0:T(8,128)S(1)} collective-permute-done((f32[8,768]{1,0:T(8,128)S(1)}, f32[8,768]{1,0:T(8,128)S(1)}, u32[]{:S(2)}, u32[]{:S(2)}) %collective-permute-start.61) | collective-permute-done | bytes 24608 | tf_op jit(solution)/shard_map/ppermute | solution.py:68
  345.8 2.8 collective-permute-start.65
  349.2 7.3 %collective-permute-done.65 = f32[8,768]{1,0:T(8,128)S(1)} collective-permute-done((f32[8,768]{1,0:T(8,128)S(1)}, f32[8,768]{1,0:T(8,128)S(1)}, u32[]{:S(2)}, u32[]{:S(2)}) %collective-permute-start.65) | collective-permute-done | bytes 24608 | tf_op jit(solution)/shard_map/ppermute | solution.py:68
  (364 shorter events, 72.9 us)
Async XLA Ops:
  7.2 139.6 %all-gather.5.cloned.1.call-start = ((), (), s32[]{:S(2)}) async-start(), calls=%async_computation.2 | async-start | bytes 7520256 | tf_op jit(solution)/shard_map/all_gather | solution.py:979
  14.3 279.2 %all-gather.7.cloned.1.call-start = ((), (), s32[]{:S(2)}) async-start(), calls=%async_computation.3 | async-start | bytes 1775616 | tf_op jit(solution)/shard_map/all_gather | solution.py:1080
  28.2 16.3 %collective-permute-start.3 = (bf16[2,96,768]{2,1,0:T(8,128)(2,1)S(1)}, bf16[2,96,768]{2,1,0:T(8,128)(2,1)S(1)}, u32[]{:S(2)}, u32[]{:S(2)}) collective-permute-start(bf16[2,96,768]{2,1,0:T(8,128)(2,1)S(1)} %constant_dynamic-update-slice_fusion), channel_id=1, source_target_pairs={{0,4},{1,5},{2,6},{3,7},{4,0},{5,1},{6,2},{7,3},{8,12},{9,13},{10,... | collective-permute-start | bytes 884744 | tf_op jit(solution)/shard_map/ppermute | solution.py:68
  44.6 25.4 %collective-permute-start.6 = (bf16[4,48,768]{2,1,0:T(8,128)(2,1)S(1)}, bf16[4,48,768]{2,1,0:T(8,128)(2,1)S(1)}, u32[]{:S(2)}, u32[]{:S(2)}) collective-permute-start(bf16[4,48,768]{2,1,0:T(8,128)(2,1)S(1)} %pad_maximum_fusion.5), channel_id=1, source_target_pairs={{0,2},{1,3},{2,0},{3,1},{4,6},{5,7},{6,4},{7,5},{8,10},{9,11},{10,... | collective-permute-start | bytes 884744 | tf_op jit(solution)/shard_map/ppermute | solution.py:68
  46.2 23.8 %collective-permute-start.5 = (bf16[4,48,768]{2,1,0:T(8,128)(2,1)S(1)}, bf16[4,48,768]{2,1,0:T(8,128)(2,1)S(1)}, u32[]{:S(2)}, u32[]{:S(2)}) collective-permute-start(bf16[4,48,768]{2,1,0:T(8,128)(2,1)S(1)} %pad_maximum_fusion.4), channel_id=1, source_target_pairs={{0,1},{1,0},{2,3},{3,2},{4,5},{5,4},{6,7},{7,6},{8,9},{9,8},{10,11... | collective-permute-start | bytes 884744 | tf_op jit(solution)/shard_map/ppermute | solution.py:68
  46.9 23.1 %collective-permute-start.7 = (bf16[1,144,768]{2,1,0:T(8,128)(2,1)S(1)}, bf16[1,144,768]{2,1,0:T(8,128)(2,1)S(1)}, u32[]{:S(2)}, u32[]{:S(2)}) collective-permute-start(bf16[1,144,768]{2,1,0:T(8,128)(2,1)S(1)} %maximum_bitcast_fusion), channel_id=1, source_target_pairs={{0,8},{1,9},{2,10},{3,11},{4,12},{5,13},{6,14},{7,15},{8,0},{9,1},... | collective-permute-start | bytes 663560 | tf_op jit(solution)/shard_map/ppermute | solution.py:68
  48.7 11.6 %collective-permute-start.8 = (bf16[4,16,768]{2,1,0:T(8,128)(2,1)S(1)}, bf16[4,16,768]{2,1,0:T(8,128)(2,1)S(1)}, u32[]{:S(2)}, u32[]{:S(2)}) collective-permute-start(bf16[4,16,768]{2,1,0:T(8,128)(2,1)S(1)} %constant_dynamic-update-slice_fusion.4), channel_id=1, source_target_pairs={{0,4},{1,5},{2,6},{3,7},{4,0},{5,1},{6,2},{7,3},{8,12},{9,13},{10,... | collective-permute-start | bytes 294920 | tf_op jit(solution)/shard_map/ppermute | solution.py:68
  70.0 20.7 %collective-permute-start.10 = (bf16[8,48,768]{2,1,0:T(8,128)(2,1)S(1)}, bf16[8,48,768]{2,1,0:T(8,128)(2,1)S(1)}, u32[]{:S(2)}, u32[]{:S(2)}) collective-permute-start(bf16[8,48,768]{2,1,0:T(8,128)(2,1)S(1)} %constant_dynamic-update-slice_fusion.8.rest_4_.rest_0_), channel_id=1, source_target_pairs={{0,1},{1,0},{2,3},{3,2},{4,5},{5,4},{6,7},{7,6},{8,9},{9,8},{10,11... | collective-permute-start | bytes 1769480 | tf_op jit(solution)/shard_map/ppermute | solution.py:68
  71.2 19.6 %collective-permute-start.9 = (bf16[8,48,768]{2,1,0:T(8,128)(2,1)S(1)}, bf16[8,48,768]{2,1,0:T(8,128)(2,1)S(1)}, u32[]{:S(2)}, u32[]{:S(2)}) collective-permute-start(bf16[8,48,768]{2,1,0:T(8,128)(2,1)S(1)} %constant_dynamic-update-slice_fusion.6.rest_0_), channel_id=1, source_target_pairs={{0,2},{1,3},{2,0},{3,1},{4,6},{5,7},{6,4},{7,5},{8,10},{9,11},{10,... | collective-permute-start | bytes 1769480 | tf_op jit(solution)/shard_map/ppermute | solution.py:68
  71.3 19.4 %collective-permute-start.11 = (bf16[2,144,768]{2,1,0:T(8,128)(2,1)S(1)}, bf16[2,144,768]{2,1,0:T(8,128)(2,1)S(1)}, u32[]{:S(2)}, u32[]{:S(2)}) collective-permute-start(bf16[2,144,768]{2,1,0:T(8,128)(2,1)S(1)} %constant_dynamic-update-slice_fusion.10), channel_id=1, source_target_pairs={{0,4},{1,5},{2,6},{3,7},{4,0},{5,1},{6,2},{7,3},{8,12},{9,13},{10,... | collective-permute-start | bytes 1327112 | tf_op jit(solution)/shard_map/ppermute | solution.py:68
  71.4 17.0 %collective-permute-start.12 = (bf16[8,16,768]{2,1,0:T(8,128)(2,1)S(1)}, bf16[8,16,768]{2,1,0:T(8,128)(2,1)S(1)}, u32[]{:S(2)}, u32[]{:S(2)}) collective-permute-start(bf16[8,16,768]{2,1,0:T(8,128)(2,1)S(1)} %constant_dynamic-update-slice_fusion.12), channel_id=1, source_target_pairs={{0,8},{1,9},{2,10},{3,11},{4,12},{5,13},{6,14},{7,15},{8,0},{9,1},... | collective-permute-start | bytes 589832 | tf_op jit(solution)/shard_map/ppermute | solution.py:68
  74.7 20.9 %collective-permute-start.18 = (bf16[8,48,768]{2,1,0:T(8,128)(2,1)S(1)}, bf16[8,48,768]{2,1,0:T(8,128)(2,1)S(1)}, u32[]{:S(2)}, u32[]{:S(2)}) collective-permute-start(bf16[8,48,768]{2,1,0:T(8,128)(2,1)S(1)} %constant_dynamic-update-slice_fusion.8.rest_4_.rest_0_), channel_id=1, source_target_pairs={{0,16},{16,0},{1,17},{17,1},{2,18},{18,2},{3,19},{19,3},{4,20},{20... | collective-permute-start | bytes 1769480 | tf_op jit(solution)/shard_map/ppermute | solution.py:63
  93.8 24.3 %collective-permute-start.14 = (bf16[4,64,768]{2,1,0:T(8,128)(2,1)S(1)}, bf16[4,64,768]{2,1,0:T(8,128)(2,1)}, u32[]{:S(2)}, u32[]{:S(2)}) collective-permute-start(bf16[4,64,768]{2,1,0:T(8,128)(2,1)S(1)} %pad_maximum_fusion.3), channel_id=1, source_target_pairs={{0,2},{1,3},{2,0},{3,1},{4,6},{5,7},{6,4},{7,5},{8,10},{9,11},{10,... | collective-permute-start | bytes 1179656 | tf_op jit(solution)/shard_map/ppermute | solution.py:68
  95.6 24.2 %collective-permute-start.13 = (bf16[4,80,768]{2,1,0:T(8,128)(2,1)S(1)}, bf16[4,80,768]{2,1,0:T(8,128)(2,1)S(1)}, u32[]{:S(2)}, u32[]{:S(2)}) collective-permute-start(bf16[4,80,768]{2,1,0:T(8,128)(2,1)S(1)} %pad_maximum_fusion.1), channel_id=1, source_target_pairs={{0,1},{1,0},{2,3},{3,2},{4,5},{5,4},{6,7},{7,6},{8,9},{9,8},{10,11... | collective-permute-start | bytes 1474568 | tf_op jit(solution)/shard_map/ppermute | solution.py:68
  121.5 25.2 %collective-permute-start.21 = (bf16[8,80,768]{2,1,0:T(8,128)(2,1)}, bf16[8,80,768]{2,1,0:T(8,128)(2,1)}, u32[]{:S(2)}, u32[]{:S(2)}) collective-permute-start(bf16[8,80,768]{2,1,0:T(8,128)(2,1)} %constant_dynamic-update-slice_fusion.16.rest_0_), channel_id=1, source_target_pairs={{0,2},{1,3},{2,0},{3,1},{4,6},{5,7},{6,4},{7,5},{8,10},{9,11},{10,... | collective-permute-start | bytes 2949128 | tf_op jit(solution)/shard_map/ppermute | solution.py:68
  123.4 23.3 %collective-permute-start.22 = (bf16[8,64,768]{2,1,0:T(8,128)(2,1)S(1)}, bf16[8,64,768]{2,1,0:T(8,128)(2,1)S(1)}, u32[]{:S(2)}, u32[]{:S(2)}) collective-permute-start(bf16[8,64,768]{2,1,0:T(8,128)(2,1)S(1)} %constant_dynamic-update-slice_fusion.18.rest_4_.rest_8_.rest_0_), channel_id=1, source_target_pairs={{0,1},{1,0},{2,3},{3,2},{4,5},{5,4},{6,7},{7,6},{8,9},{9,8},{10,11... | collective-permute-start | bytes 2359304 | tf_op jit(solution)/shard_map/ppermute | solution.py:68
  157.7 17.1 %collective-permute-start.28 = (bf16[16,288,768]{2,1,0:T(8,128)(2,1)}, bf16[16,288,768]{2,1,0:T(8,128)(2,1)}, u32[]{:S(2)}, u32[]{:S(2)}) collective-permute-start(bf16[16,288,768]{2,1,0:T(8,128)(2,1)} %bitcast.103), channel_id=1, source_target_pairs={{0,16},{16,0},{1,17},{17,1},{2,18},{18,2},{3,19},{19,3},{4,20},{20... | collective-permute-start | bytes 21233672 | tf_op jit(solution)/shard_map/ppermute | solution.py:63
  157.9 16.9 %collective-permute-start.32 = (bf16[384,1536]{1,0:T(8,128)(2,1)S(1)}, bf16[384,1536]{1,0:T(8,128)(2,1)S(1)}, u32[]{:S(2)}, u32[]{:S(2)}) collective-permute-start(bf16[384,1536]{1,0:T(8,128)(2,1)S(1)} %pad_maximum_fusion.self_own.rest_8_), channel_id=1, source_target_pairs={{0,16},{16,0},{1,17},{17,1},{2,18},{18,2},{3,19},{19,3},{4,20},{20... | collective-permute-start | bytes 3538952 | tf_op jit(solution)/shard_map/ppermute | solution.py:63
  158.2 16.5 %collective-permute-start.29 = (bf16[512,768]{1,0:T(8,128)(2,1)}, bf16[512,768]{1,0:T(8,128)(2,1)S(1)}, u32[]{:S(2)}, u32[]{:S(2)}) collective-permute-start(bf16[512,768]{1,0:T(8,128)(2,1)} %get-tuple-element.265.n1), channel_id=1, source_target_pairs={{0,16},{16,0},{1,17},{17,1},{2,18},{18,2},{3,19},{19,3},{4,20},{20... | collective-permute-start | bytes 2359304 | tf_op jit(solution)/shard_map/ppermute | solution.py:63
  158.4 16.4 %collective-permute-start.30 = (bf16[512,768]{1,0:T(8,128)(2,1)}, bf16[512,768]{1,0:T(8,128)(2,1)}, u32[]{:S(2)}, u32[]{:S(2)}) collective-permute-start(bf16[512,768]{1,0:T(8,128)(2,1)} %get-tuple-element.277.c), channel_id=1, source_target_pairs={{0,16},{16,0},{1,17},{17,1},{2,18},{18,2},{3,19},{19,3},{4,20},{20... | collective-permute-start | bytes 2359304 | tf_op jit(solution)/shard_map/ppermute | solution.py:63
  158.7 16.0 %collective-permute-start.31 = (bf16[512,768]{1,0:T(8,128)(2,1)}, bf16[512,768]{1,0:T(8,128)(2,1)S(1)}, u32[]{:S(2)}, u32[]{:S(2)}) collective-permute-start(bf16[512,768]{1,0:T(8,128)(2,1)} %get-tuple-element.329.n2), channel_id=1, source_target_pairs={{0,16},{16,0},{1,17},{17,1},{2,18},{18,2},{3,19},{19,3},{4,20},{20... | collective-permute-start | bytes 2359304 | tf_op jit(solution)/shard_map/ppermute | solution.py:63
  181.0 27.6 %collective-permute-start.35 = (bf16[512,3072]{1,0:T(8,128)(2,1)}, bf16[512,3072]{1,0:T(8,128)(2,1)S(1)}, u32[]{:S(2)}, u32[]{:S(2)}) collective-permute-start(bf16[512,3072]{1,0:T(8,128)(2,1)} %get-tuple-element.316.f), channel_id=1, source_target_pairs={{0,16},{16,0},{1,17},{17,1},{2,18},{18,2},{3,19},{19,3},{4,20},{20... | collective-permute-start | bytes 9437192 | tf_op jit(solution)/shard_map/ppermute | solution.py:63
  202.0 16.5 %collective-permute-start.36 = (bf16[512,1536]{1,0:T(8,128)(2,1)}, bf16[512,1536]{1,0:T(8,128)(2,1)S(1)}, u32[]{:S(2)}, u32[]{:S(2)}) collective-permute-start(bf16[512,1536]{1,0:T(8,128)(2,1)} %get-tuple-element.322), channel_id=1, source_target_pairs={{0,16},{16,0},{1,17},{17,1},{2,18},{18,2},{3,19},{19,3},{4,20},{20... | collective-permute-start | bytes 4718600 | tf_op jit(solution)/shard_map/ppermute | solution.py:63
  208.7 11.9 %collective-permute-start.47 = (bf16[8,6528]{1,0:T(8,128)(2,1)}, bf16[8,6528]{1,0:T(8,128)(2,1)S(1)}, u32[]{:S(2)}, u32[]{:S(2)}) collective-permute-start(bf16[8,6528]{1,0:T(8,128)(2,1)} %get-tuple-element.375), channel_id=1, source_target_pairs={{0,16},{16,0},{1,17},{17,1},{2,18},{18,2},{3,19},{19,3},{4,20},{20... | collective-permute-start | bytes 313352 | tf_op jit(solution)/shard_map/ppermute | solution.py:63
  218.5 21.8 %collective-permute-start.37 = (bf16[8,48,768]{2,1,0:T(8,128)(2,1)}, bf16[8,48,768]{2,1,0:T(8,128)(2,1)S(1)}, u32[]{:S(2)}, u32[]{:S(2)}) collective-permute-start(bf16[8,48,768]{2,1,0:T(8,128)(2,1)} %get-tuple-element.324), channel_id=1, source_target_pairs={{0,2},{1,3},{2,0},{3,1},{4,6},{5,7},{6,4},{7,5},{8,10},{9,11},{10,... | collective-permute-start | bytes 1769480 | tf_op jit(solution)/shard_map/ppermute | solution.py:68
  219.9 20.4 %collective-permute-start.38 = (bf16[8,48,768]{2,1,0:T(8,128)(2,1)}, bf16[8,48,768]{2,1,0:T(8,128)(2,1)S(1)}, u32[]{:S(2)}, u32[]{:S(2)}) collective-permute-start(bf16[8,48,768]{2,1,0:T(8,128)(2,1)} %get-tuple-element.326), channel_id=1, source_target_pairs={{0,1},{1,0},{2,3},{3,2},{4,5},{5,4},{6,7},{7,6},{8,9},{9,8},{10,11... | collective-permute-start | bytes 1769480 | tf_op jit(solution)/shard_map/ppermute | solution.py:68
  227.9 40.4 %collective-permute-start.41 = (bf16[8,96,768]{2,1,0:T(8,128)(2,1)}, bf16[8,96,768]{2,1,0:T(8,128)(2,1)S(1)}, u32[]{:S(2)}, u32[]{:S(2)}) collective-permute-start(bf16[8,96,768]{2,1,0:T(8,128)(2,1)} %get-tuple-element.344), channel_id=1, source_target_pairs={{0,2},{1,3},{2,0},{3,1},{4,6},{5,7},{6,4},{7,5},{8,10},{9,11},{10,... | collective-permute-start | bytes 3538952 | tf_op jit(solution)/shard_map/ppermute | solution.py:68
  239.6 27.0 %collective-permute-start.42 = (bf16[8,48,768]{2,1,0:T(8,128)(2,1)}, bf16[8,48,768]{2,1,0:T(8,128)(2,1)S(1)}, u32[]{:S(2)}, u32[]{:S(2)}) collective-permute-start(bf16[8,48,768]{2,1,0:T(8,128)(2,1)} %get-tuple-element.346), channel_id=1, source_target_pairs={{0,1},{1,0},{2,3},{3,2},{4,5},{5,4},{6,7},{7,6},{8,9},{9,8},{10,11... | collective-permute-start | bytes 1769480 | tf_op jit(solution)/shard_map/ppermute | solution.py:68
  240.4 27.9 %collective-permute-start.40 = (bf16[4,48,768]{2,1,0:T(8,128)(2,1)S(1)}, bf16[4,48,768]{2,1,0:T(8,128)(2,1)S(1)}, u32[]{:S(2)}, u32[]{:S(2)}) collective-permute-start(bf16[4,48,768]{2,1,0:T(8,128)(2,1)S(1)} %get-tuple-element.462), channel_id=1, source_target_pairs={{0,2},{1,3},{2,0},{3,1},{4,6},{5,7},{6,4},{7,5},{8,10},{9,11},{10,... | collective-permute-start | bytes 884744 | tf_op jit(solution)/shard_map/ppermute | solution.py:68
  242.1 26.3 %collective-permute-start.39 = (bf16[4,48,768]{2,1,0:T(8,128)(2,1)S(1)}, bf16[4,48,768]{2,1,0:T(8,128)(2,1)S(1)}, u32[]{:S(2)}, u32[]{:S(2)}) collective-permute-start(bf16[4,48,768]{2,1,0:T(8,128)(2,1)S(1)} %get-tuple-element.464), channel_id=1, source_target_pairs={{0,1},{1,0},{2,3},{3,2},{4,5},{5,4},{6,7},{7,6},{8,9},{9,8},{10,11... | collective-permute-start | bytes 884744 | tf_op jit(solution)/shard_map/ppermute | solution.py:68
  268.4 17.0 %collective-permute-start.44 = (bf16[2,512,768]{2,1,0:T(8,128)(2,1)}, bf16[2,512,768]{2,1,0:T(8,128)(2,1)}, u32[]{:S(2)}, u32[]{:S(2)}) collective-permute-start(bf16[2,512,768]{2,1,0:T(8,128)(2,1)} %get-tuple-element.358), channel_id=1, source_target_pairs={{0,16},{16,0},{1,17},{17,1},{2,18},{18,2},{3,19},{19,3},{4,20},{20... | collective-permute-start | bytes 4718600 | tf_op jit(solution)/shard_map/ppermute | solution.py:63
  269.5 23.9 %collective-permute-start.45 = (bf16[4,96,768]{2,1,0:T(8,128)(2,1)}, bf16[4,96,768]{2,1,0:T(8,128)(2,1)}, u32[]{:S(2)}, u32[]{:S(2)}) collective-permute-start(bf16[4,96,768]{2,1,0:T(8,128)(2,1)} %get-tuple-element.448), channel_id=1, source_target_pairs={{0,1},{1,0},{2,3},{3,2},{4,5},{5,4},{6,7},{7,6},{8,9},{9,8},{10,11... | collective-permute-start | bytes 1769480 | tf_op jit(solution)/shard_map/ppermute | solution.py:68
  271.7 13.7 %collective-permute-start.43 = (bf16[2,96,768]{2,1,0:T(8,128)(2,1)}, bf16[2,96,768]{2,1,0:T(8,128)(2,1)S(1)}, u32[]{:S(2)}, u32[]{:S(2)}) collective-permute-start(bf16[2,96,768]{2,1,0:T(8,128)(2,1)} %get-tuple-element.460), channel_id=1, source_target_pairs={{0,4},{1,5},{2,6},{3,7},{4,0},{5,1},{6,2},{7,3},{8,12},{9,13},{10,... | collective-permute-start | bytes 884744 | tf_op jit(solution)/shard_map/ppermute | solution.py:68
  273.3 20.1 %collective-permute-start.46 = (bf16[4,48,768]{2,1,0:T(8,128)(2,1)S(1)}, bf16[4,48,768]{2,1,0:T(8,128)(2,1)S(1)}, u32[]{:S(2)}, u32[]{:S(2)}) collective-permute-start(bf16[4,48,768]{2,1,0:T(8,128)(2,1)S(1)} %get-tuple-element.458), channel_id=1, source_target_pairs={{0,2},{1,3},{2,0},{3,1},{4,6},{5,7},{6,4},{7,5},{8,10},{9,11},{10,... | collective-permute-start | bytes 884744 | tf_op jit(solution)/shard_map/ppermute | solution.py:68
  293.4 11.2 %collective-permute-start.54 = (bf16[128,6528]{1,0:T(8,128)(2,1)}, bf16[128,6528]{1,0:T(8,128)(2,1)}, u32[]{:S(2)}, u32[]{:S(2)}) collective-permute-start(bf16[128,6528]{1,0:T(8,128)(2,1)} %all-gather.7.cloned.1.call-done.own), channel_id=1, source_target_pairs={{0,16},{16,0},{1,17},{17,1},{2,18},{18,2},{3,19},{19,3},{4,20},{20... | collective-permute-start | bytes 5013512 | tf_op jit(solution)/shard_map/ppermute | solution.py:63
  298.9 17.5 %collective-permute-start.51 = (bf16[2,144,768]{2,1,0:T(8,128)(2,1)S(1)}, bf16[2,144,768]{2,1,0:T(8,128)(2,1)S(1)}, u32[]{:S(2)}, u32[]{:S(2)}) collective-permute-start(bf16[2,144,768]{2,1,0:T(8,128)(2,1)S(1)} %get-tuple-element.450), channel_id=1, source_target_pairs={{0,4},{1,5},{2,6},{3,7},{4,0},{5,1},{6,2},{7,3},{8,12},{9,13},{10,... | collective-permute-start | bytes 1327112 | tf_op jit(solution)/shard_map/ppermute | solution.py:68
  299.7 16.6 %collective-permute-start.49 = (bf16[8,48,768]{2,1,0:T(8,128)(2,1)}, bf16[8,48,768]{2,1,0:T(8,128)(2,1)S(1)}, u32[]{:S(2)}, u32[]{:S(2)}) collective-permute-start(bf16[8,48,768]{2,1,0:T(8,128)(2,1)} %get-tuple-element.383), channel_id=1, source_target_pairs={{0,2},{1,3},{2,0},{3,1},{4,6},{5,7},{6,4},{7,5},{8,10},{9,11},{10,... | collective-permute-start | bytes 1769480 | tf_op jit(solution)/shard_map/ppermute | solution.py:68
  300.7 15.7 %collective-permute-start.50 = (bf16[8,48,768]{2,1,0:T(8,128)(2,1)S(1)}, bf16[8,48,768]{2,1,0:T(8,128)(2,1)S(1)}, u32[]{:S(2)}, u32[]{:S(2)}) collective-permute-start(bf16[8,48,768]{2,1,0:T(8,128)(2,1)S(1)} %copy-done.52), channel_id=1, source_target_pairs={{0,1},{1,0},{2,3},{3,2},{4,5},{5,4},{6,7},{7,6},{8,9},{9,8},{10,11... | collective-permute-start | bytes 1769480 | tf_op jit(solution)/shard_map/ppermute | solution.py:68
  301.9 11.0 %collective-permute-start.52 = (bf16[1,96,768]{2,1,0:T(8,128)(2,1)S(1)}, bf16[1,96,768]{2,1,0:T(8,128)(2,1)S(1)}, u32[]{:S(2)}, u32[]{:S(2)}) collective-permute-start(bf16[1,96,768]{2,1,0:T(8,128)(2,1)S(1)} %get-tuple-element.468), channel_id=1, source_target_pairs={{0,8},{1,9},{2,10},{3,11},{4,12},{5,13},{6,14},{7,15},{8,0},{9,1},... | collective-permute-start | bytes 442376 | tf_op jit(solution)/shard_map/ppermute | solution.py:68
  304.7 11.7 %collective-permute-start.53 = (f32[8,768]{1,0:T(8,128)S(1)}, f32[8,768]{1,0:T(8,128)S(1)}, u32[]{:S(2)}, u32[]{:S(2)}) collective-permute-start(f32[8,768]{1,0:T(8,128)S(1)} %add.202), channel_id=1, source_target_pairs={{0,1},{1,0},{2,3},{3,2},{4,5},{5,4},{6,7},{7,6},{8,9},{9,8},{10,11... | collective-permute-start | bytes 73736 | tf_op jit(solution)/shard_map/ppermute | solution.py:68
  316.4 17.8 %collective-permute-start.69 = (bf16[96,768]{1,0:T(8,128)(2,1)S(1)}, bf16[96,768]{1,0:T(8,128)(2,1)S(1)}, u32[]{:S(2)}, u32[]{:S(2)}) collective-permute-start(bf16[96,768]{1,0:T(8,128)(2,1)S(1)} %get-tuple-element.481), channel_id=1, source_target_pairs={{0,16},{16,0},{1,17},{17,1},{2,18},{18,2},{3,19},{19,3},{4,20},{20... | collective-permute-start | bytes 442376 | tf_op jit(solution)/shard_map/ppermute | solution.py:63
  321.1 16.6 %collective-permute-start.60 = (bf16[1,144,768]{2,1,0:T(8,128)(2,1)}, bf16[1,144,768]{2,1,0:T(8,128)(2,1)}, u32[]{:S(2)}, u32[]{:S(2)}) collective-permute-start(bf16[1,144,768]{2,1,0:T(8,128)(2,1)} %get-tuple-element.466), channel_id=1, source_target_pairs={{0,8},{1,9},{2,10},{3,11},{4,12},{5,13},{6,14},{7,15},{8,0},{9,1},... | collective-permute-start | bytes 663560 | tf_op jit(solution)/shard_map/ppermute | solution.py:68
  328.1 15.2 %collective-permute-start.59 = (bf16[2,96,768]{2,1,0:T(8,128)(2,1)S(1)}, bf16[2,96,768]{2,1,0:T(8,128)(2,1)S(1)}, u32[]{:S(2)}, u32[]{:S(2)}) collective-permute-start(bf16[2,96,768]{2,1,0:T(8,128)(2,1)S(1)} %get-tuple-element.452), channel_id=1, source_target_pairs={{0,4},{1,5},{2,6},{3,7},{4,0},{5,1},{6,2},{7,3},{8,12},{9,13},{10,... | collective-permute-start | bytes 884744 | tf_op jit(solution)/shard_map/ppermute | solution.py:68
  329.8 14.0 %all-to-all-start.1 = ((bf16[16,8,768]{2,1,0:T(8,128)(2,1)}), bf16[16,8,768]{2,1,0:T(8,128)(2,1)S(1)}, u32[]{:S(2)}, u32[]{:S(2)}) async-start(bf16[16,8,768]{2,1,0:T(8,128)(2,1)} %bitcast.31), calls=%async_computation.1 | async-start | bytes 393216 | tf_op jit(solution)/shard_map/all_to_all | solution.py:1128
  337.1 21.4 %collective-permute-start.63 = (bf16[512,384]{1,0:T(8,128)(2,1)}, bf16[512,384]{1,0:T(8,128)(2,1)S(1)}, u32[]{:S(2)}, u32[]{:S(2)}) collective-permute-start(bf16[512,384]{1,0:T(8,128)(2,1)} %get-tuple-element.414), channel_id=1, source_target_pairs={{0,16},{16,0},{1,17},{17,1},{2,18},{18,2},{3,19},{19,3},{4,20},{20... | collective-permute-start | bytes 1179656 | tf_op jit(solution)/shard_map/ppermute | solution.py:63
  344.8 15.7 %collective-permute-start.68 = (bf16[144,768]{1,0:T(8,128)(2,1)S(1)}, bf16[144,768]{1,0:T(8,128)(2,1)S(1)}, u32[]{:S(2)}, u32[]{:S(2)}) collective-permute-start(bf16[144,768]{1,0:T(8,128)(2,1)S(1)} %get-tuple-element.473), channel_id=1, source_target_pairs={{0,16},{16,0},{1,17},{17,1},{2,18},{18,2},{3,19},{19,3},{4,20},{20... | collective-permute-start | bytes 663560 | tf_op jit(solution)/shard_map/ppermute | solution.py:63
  345.6 14.0 %collective-permute-start.66 = (bf16[1,96,768]{2,1,0:T(8,128)(2,1)S(1)}, bf16[1,96,768]{2,1,0:T(8,128)(2,1)S(1)}, u32[]{:S(2)}, u32[]{:S(2)}) collective-permute-start(bf16[1,96,768]{2,1,0:T(8,128)(2,1)S(1)} %add_convert_fusion.20), channel_id=1, source_target_pairs={{0,8},{1,9},{2,10},{3,11},{4,12},{5,13},{6,14},{7,15},{8,0},{9,1},... | collective-permute-start | bytes 442376 | tf_op jit(solution)/shard_map/ppermute | solution.py:68
  345.8 10.7 %collective-permute-start.65 = (f32[8,768]{1,0:T(8,128)S(1)}, f32[8,768]{1,0:T(8,128)S(1)}, u32[]{:S(2)}, u32[]{:S(2)}) collective-permute-start(f32[8,768]{1,0:T(8,128)S(1)} %add.220), channel_id=1, source_target_pairs={{0,8},{1,9},{2,10},{3,11},{4,12},{5,13},{6,14},{7,15},{8,0},{9,1},... | collective-permute-start | bytes 73736 | tf_op jit(solution)/shard_map/ppermute | solution.py:68
  (81 other events, 559.2 us)
Sparse Core Ops, SparseCore 0:
  14.4 131.9 all-gather.4
  221.4 62.7 all-gather.6
where the time goes:
time: 377 us; the launch traced here: 370 us
  Pallas kernels  138 us (37%)
  waiting for transfers between devices  91.7 us (24%)
  starting transfers between devices  65.1 us (17%)
  local copies, waits for them, and re-layouts  20.9 us (6%)
  blocking collectives  20.5 us (5%)
  other arithmetic  16.8 us (4%)
  between operations  16 us (4%)
    pallas_call x14, Pallas kernels, call(): pl.pallas_call(body, name=name, out_shape=[jax.ShapeDtypeStruct(s, k) for...  138 us
    ppermute x38, waiting for transfers between devices, along(): return lax.ppermute(value, 'dp', [(i, i ^ 1 << bit) for i in range(count)])  80.4 us
    ppermute x38, starting transfers between devices, along(): return lax.ppermute(value, 'dp', [(i, i ^ 1 << bit) for i in range(count)])  53 us
    all_to_all x1, blocking collectives, per_device(): gw = lax.all_to_all(gw, 'dp', 0, 0)  20.5 us
    ppermute x32, waiting for transfers between devices, across(): return lax.ppermute(value, 'section', [(0, 1), (1, 0)])  10.7 us
    ppermute x32, starting transfers between devices, across(): return lax.ppermute(value, 'section', [(0, 1), (1, 0)])  7.66 us
  transfers between devices with their start and end apart: 73, of which 24 were waited for; matrix products, arithmetic and copies ran while one was open for 8% of the time, Pallas kernels for 35%

commit v1 on v0

--- a/solution.py
+++ b/solution.py
@@ -199,10 +199,10 @@
 
 def gelu_both(u):
     c = 0.7978845608028654
-    t = jnp.tanh(c * (u + 0.044715 * u * u * u))
-    value = 0.5 * u * (1.0 + t)
-    slope = 0.5 * (1.0 + t) + (0.5 * c) * u * (1.0 - t * t) * (1.0 + 3 * 0.044715 * u * u)
-    return value, slope
+    square = u * u
+    half = 0.5 + 0.5 * jnp.tanh(u * (c + (0.044715 * c) * square))
+    value = u * half
+    return value, half + value * (1.0 - half) * (2.0 * c + (6.0 * 0.044715 * c) * square)
 
 
 def square_row(b):
@@ -240,10 +240,12 @@
     return [part for sets, items in sources for part, ids, other in sets]
 
 
-def start_sources(meta, refs, sources, dst, sems):
+def start_sources(meta, refs, sources, dst, sems, turn=None):
     at = 0
-    for sets, items in sources:
+    for k, (sets, items) in enumerate(sources):
         plan = [(ids, other) for part, ids, other in sets]
+        if turn is not None:
+            items = (items[:1] if turn == 0 else items[1:]) if k == 0 else items * turn
         start_fetch(meta, refs[at : at + len(plan)], plan, items, dst, sems)
         at += len(plan)
 
@@ -267,6 +269,10 @@
                 off = pl.multiple_of(row_of(source, group), 16)
                 at = sem.at[sem_of[0](source, group)] if sem_of else sem
                 pltpu.make_async_copy(ref.at[slot, pl.ds(first, count)], dst.at[pl.ds(off, count)], at).start()
+
+
+def start_copy(src, dst, sem):
+    pltpu.make_async_copy(src, dst, sem).start()
 
 
 def drain(ref, sem):
@@ -362,51 +368,54 @@
     return [part for part, ids, other in sets], [(ids, other) for part, ids, other in sets]
 
 
+def bias_block(tiles, h, ib):
+    return jnp.concatenate([
+        jnp.concatenate([tiles[h, min(max(jb - (2 * ib + i), -2), 2) + 2] for i in range(2)], axis=1)
+        for jb in range(ROW_LEN // TILE)
+    ], axis=0)
+
+
 def enc_attention(meta, x, gains, segr, segc, windows, a_sets, b_sets):
     a_arrays, a_plan = plan_of(a_sets)
     b_arrays, b_plan = plan_of(b_sets)
     n = len(a_arrays)
+    wide = 2 * TILE
 
     def body(meta, x, gains, segr, segc, windows, *rest):
         a_parts, b_parts, rest = rest[:n], rest[n : 2 * n], rest[2 * n :]
-        n1, q, k, v, c, h1, n2, lse, w, tiles, lcol, sems = rest
+        n1, q, k, v, c, h1, n2, lse, w, tiles, sems = rest
         start_fetch(meta, a_parts, a_plan, [(0, GROUP, square_row(0))], w, sems.at[0])
         start_fetch(meta, b_parts, b_plan, [(0, GROUP, square_row(1))], w, sems.at[0])
-        fill_bias(windows, tiles, False)
+        fill_bias(windows, tiles, True)
         xf = x[...].astype(F32)
         n1[...] = rms(xf, gains[0:1, :]).astype(BF)
         drain(w, sems.at[0])
         for ref, at in ((q, 0), (k, 2), (v, 3)):
             ref[...] = nn(n1[...], w[at * D : (at + 1) * D, :]).astype(BF)
-        lane = lax.broadcasted_iota(jnp.int32, (1, TILE), 1)
-        lcol[...] = jnp.zeros_like(lcol)
+        lse[...] = jnp.zeros_like(lse)
 
         def pair(pr, carry):
             cols = pl.ds(pl.multiple_of(pr * TILE, TILE), TILE)
-            kp, vp = k[:, cols], v[:, cols]
-            for ib in range(ROW_LEN // TILE):
-                rows = slice(ib * TILE, (ib + 1) * TILE)
-                same = segc[rows, :] == segr[...]
-                qp = q[rows, cols]
-                total = jnp.zeros((TILE, TILE), F32)
+            for ib in range(ROW_LEN // wide):
+                rows = slice(ib * wide, (ib + 1) * wide)
+                same = segc[...] == segr[:, rows]
+                total = None
                 for hh in range(2):
                     h = 2 * pr + hh
                     lanes = pair_lanes(hh)
-                    bias = jnp.concatenate(
-                        [tiles[h, min(max(jb - ib, -2), 2) + 2] for jb in range(ROW_LEN // TILE)], axis=1
-                    )
-                    s = jnp.where(same, nt(masked(qp, lanes), kp) + bias, MASKED)
-                    top = jnp.max(s, axis=-1, keepdims=True)
+                    s = nt(masked(k[:, cols], lanes), q[rows, cols]) + bias_block(tiles, h, ib)
+                    s = jnp.where(same, s, MASKED)
+                    top = jnp.max(s, axis=0, keepdims=True)
                     ex = jnp.exp(s - top)
-                    tot = jnp.sum(ex, axis=-1, keepdims=True)
+                    tot = jnp.sum(ex, axis=0, keepdims=True)
                     p = (ex * (1.0 / tot)).astype(BF)
-                    total = total + nn(p, masked(vp, lanes))
-                    lcol[rows, :] = jnp.where(lane == h, top + jnp.log(tot), lcol[rows, :])
+                    part = tn(p, masked(v[:, cols], lanes))
+                    total = part if total is None else total + part
+                    lse[pl.ds(h, 1), rows] = top + jnp.log(tot)
                 c[rows, cols] = total.astype(BF)
             return carry
 
         lax.fori_loop(0, HEADS // 2, pair, 0)
-        lse[...] = lcol[...].T
         res = x[...].astype(F32) + nn(c[...], w[D : 2 * D, :])
         h1[...] = res
         n2[...] = rms(res, gains[1:2, :]).astype(BF)
@@ -416,8 +425,56 @@
         body, "enc_attention", [meta, x, gains, segr, segc, windows, *a_arrays, *b_arrays],
         [SM, VM, VM, VM, VM, VM] + [ANY] * (2 * n),
         [(rows, BF)] * 5 + [(rows, F32), (rows, BF), ((TILE, ROW_LEN), F32), ], [VM] * 8,
-        [pltpu.VMEM((4 * D, D), BF), pltpu.VMEM((HEADS, 5, TILE, TILE), F32), pltpu.VMEM((ROW_LEN, TILE), F32), pltpu.SemaphoreType.DMA((2,))],
+        [pltpu.VMEM((4 * D, D), BF), pltpu.VMEM((HEADS, 5, TILE, TILE), F32), pltpu.SemaphoreType.DMA((2,))],
         us=20,
+    )
+
+
+PART = (GROUPS // 2, GROUP, D)
+WIDE_PART = (GROUPS // 2, 2 * GROUP, D)
+BLOCKS = FF // D
+
+
+def enc_ffn(meta, h1, n2, w_in_from, w_back_from):
+    in_arrays, back_arrays = arrays_of(w_in_from), arrays_of(w_back_from)
+    n, m = len(in_arrays), len(back_arrays)
+
+    def body(meta, h1, n2, *rest):
+        ins, backs, rest = rest[:n], rest[n : n + m], rest[n + m :]
+        f_out, slope_out, e, w_in, w_back, acc, normed, f, slope, sems = rest
+        start_copy(n2, normed, sems.at[8])
+        start_sources(meta, ins, w_in_from, w_in, sems)
+        start_copy(h1, acc, sems.at[9])
+        start_sources(meta, backs, w_back_from, w_back, sems.at[pl.ds(4, 4)])
+        drain(normed, sems.at[8])
+        for at, b in enumerate((0, 2, 1, 3)):
+            rows = slice(b * D, (b + 1) * D)
+            slot = at % 2
+            drain(w_in.at[rows], sems.at[b])
+            value, grad = gelu_both(nn(normed[...], w_in[rows, :]))
+            if at >= 2:
+                drain(f.at[slot], sems.at[10 + slot])
+                drain(slope.at[slot], sems.at[12 + slot])
+            f[slot] = value.astype(BF)
+            start_copy(f.at[slot], f_out.at[:, rows], sems.at[10 + slot])
+            slope[slot] = grad.astype(BF)
+            start_copy(slope.at[slot], slope_out.at[:, rows], sems.at[12 + slot])
+            if at == 0:
+                drain(acc, sems.at[9])
+            drain(w_back.at[rows], sems.at[4 + b])
+            acc[...] += nn(f[slot], w_back[rows, :])
+        e[...] = acc[...].astype(BF)
+        for slot in range(2):
+            drain(f.at[slot], sems.at[10 + slot])
+            drain(slope.at[slot], sems.at[12 + slot])
+
+    block = (2, ROW_LEN, D)
+    return call(
+        body, "enc_ffn", [meta, h1, n2, *in_arrays, *back_arrays], [SM, ANY, ANY] + [ANY] * (n + m),
+        [((ROW_LEN, FF), BF), ((ROW_LEN, FF), BF), ((ROW_LEN, D), BF)], [ANY, ANY, VM],
+        [pltpu.VMEM((FF, D), BF), pltpu.VMEM((FF, D), BF), pltpu.VMEM((ROW_LEN, D), F32), pltpu.VMEM((ROW_LEN, D), BF),
+         pltpu.VMEM(block, BF), pltpu.VMEM(block, BF), pltpu.SemaphoreType.DMA((14,))],
+        us=15,
     )
 
 
@@ -467,42 +524,50 @@
 
     def body(meta, de, slope, *rest):
         parts, rest = rest[:n], rest[n:]
-        du, other, w, sems = rest
-        b = pl.program_id(0)
-
-        @pl.when(b == 0)
-        def _():
-            start_sources(meta, parts, w_back_from, w, sems)
-
-        rows = pl.ds(pl.multiple_of(b * D, D), D)
-        drain(w.at[rows], sems.at[b])
-        value = (slope[...].astype(F32) * nt(de[...], w[rows, :])).astype(BF)
-        du[...] = value
-
-        @pl.when(meta[1] != b // 2)
-        def _():
-            other[:, pl.ds(pl.multiple_of(b % 2 * D, D), D)] = value
-
-    block = pl.BlockSpec((ROW_LEN, D), lambda b, meta: (0, b))
-    return call(
-        body, "enc_hidden_grad", [meta, de, slope, *arrays], [SM, VM, block] + [ANY] * n,
-        [((ROW_LEN, FF), BF), ((ROW_LEN, FF // 2), BF)], [block, VM],
-        [pltpu.VMEM((FF, D), BF), pltpu.SemaphoreType.DMA((4,))],
-        us=8, grid=(BLOCKS,),
+        du_out, other, w, slopes, du, sems = rest
+        start_sources(meta, parts, w_back_from, w, sems)
+        for b in range(BLOCKS):
+            start_copy(slope.at[:, b * D : (b + 1) * D], slopes.at[b], sems.at[4 + b])
+        for b in range(BLOCKS):
+            cols = slice(b * D, (b + 1) * D)
+            drain(w.at[cols], sems.at[b])
+            drain(slopes.at[b], sems.at[4 + b])
+            du[b] = (slopes[b].astype(F32) * nt(de[...], w[cols, :])).astype(BF)
+            start_copy(du.at[b], du_out.at[:, cols], sems.at[8])
+
+            @pl.when(meta[1] != b // 2)
+            def _():
+                start_copy(du.at[b], other.at[:, (b % 2) * D : (b % 2 + 1) * D], sems.at[9])
+
+        drain(du, sems.at[8])
+        drain(du.at[pl.ds(0, 2)], sems.at[9])
+
+    block = (BLOCKS, ROW_LEN, D)
+    return call(
+        body, "enc_hidden_grad", [meta, de, slope, *arrays], [SM, VM, ANY] + [ANY] * n,
+        [((ROW_LEN, FF), BF), ((ROW_LEN, FF // 2), BF)], [ANY, ANY],
+        [pltpu.VMEM((FF, D), BF), pltpu.VMEM(block, BF), pltpu.VMEM(block, BF), pltpu.SemaphoreType.DMA((10,))],
+        us=8,
     )
 
 
 def enc_w_back_grad(meta, de, de_got, f, f_got):
     half = D // 2
 
-    def body(meta, de, de_got, f, f_got, keep_a, send_a, keep_b, send_b, mine, buf, sems):
-        mine[...] = de[:, pl.ds(pl.multiple_of(meta[1] * half, TILE), half)]
-        for b in range(FF // D):
-            cols = slice(b * D, (b + 1) * D)
+    def body(meta, de, de_got, f, f_got, keep_a, send_a, keep_b, send_b, mine, theirs, fs, buf, sems):
+        start_copy(de.at[:, pl.ds(pl.multiple_of(meta[1] * half, TILE), half)], mine, sems.at[2])
+        start_copy(de_got, theirs, sems.at[3])
+        for b in range(BLOCKS):
+            for k, ref in enumerate((f, f_got)):
+                start_copy(ref.at[:, b * D : (b + 1) * D], fs.at[b, k], sems.at[4 + b])
+        drain(mine, sems.at[2])
+        drain(theirs, sems.at[3])
+        for b in range(BLOCKS):
             at = b % 2
             if b >= 2:
                 drain(buf.at[at], sems.at[at])
-            buf[at] = (tn(f[:, cols], mine[...]) + tn(f_got[:, cols], de_got[...])).astype(BF)
+            drain(fs.at[b], sems.at[4 + b])
+            buf[at] = (tn(fs[b, 0], mine[...]) + tn(fs[b, 1], theirs[...])).astype(BF)
             for k in range(D // GROUP):
                 group, piece = b * (D // GROUP // 4) + k // 4, k % 4
                 keep, send = (keep_a, send_a) if piece < 2 else (keep_b, send_b)
@@ -511,10 +576,11 @@
         drain(buf.at[0], sems.at[0])
         drain(buf.at[1], sems.at[1])
 
-    return call(
-        body, "enc_w_back_grad", [meta, de, de_got, f, f_got], [SM] + [VM] * 4,
+    part = pltpu.VMEM((ROW_LEN, half), BF)
+    return call(
+        body, "enc_w_back_grad", [meta, de, de_got, f, f_got], [SM] + [ANY] * 4,
         [(PART, BF)] * 4, [ANY] * 4,
-        [pltpu.VMEM((ROW_LEN, half), BF), pltpu.VMEM((2, D, half), BF), pltpu.SemaphoreType.DMA((2,))],
+        [part, part, pltpu.VMEM((BLOCKS, 2, ROW_LEN, D), BF), pltpu.VMEM((2, D, half), BF), pltpu.SemaphoreType.DMA((8,))],
         us=7,
     )
 
@@ -545,24 +611,33 @@
 
     def body(meta, du, h1, de, gains, *rest):
         parts, rest = rest[:n], rest[n:]
-        dh1, da, dgain, w, acc, sems = rest
-        start_sources(meta, parts, w_in_from, w, sems)
+        dh1, da, dgain, w, acc, dus, h1s, des, sems = rest
+        for first in range(2):
+            for b in (first, first + 2):
+                start_copy(du.at[:, b * D : (b + 1) * D], dus.at[b], sems.at[4 + b])
+            start_sources(meta, parts, w_in_from, w, sems, first)
+        start_copy(h1, h1s, sems.at[8])
+        start_copy(de, des, sems.at[9])
         for k, b in enumerate((0, 2, 1, 3)):
             cols = slice(b * D, (b + 1) * D)
             drain(w.at[cols], sems.at[b])
-            part = nt(du[:, cols], w[cols, :])
+            drain(dus.at[b], sems.at[4 + b])
+            part = nt(dus[b], w[cols, :])
             acc[...] = part if k == 0 else acc[...] + part
-        dv, dg = rms_back(h1[...], gains[1:2, :], acc[...])
-        total = de[...].astype(F32) + dv
+        drain(h1s, sems.at[8])
+        drain(des, sems.at[9])
+        dv, dg = rms_back(h1s[...], gains[1:2, :], acc[...])
+        total = des[...].astype(F32) + dv
         dh1[...] = total
         da[...] = total.astype(BF)
         dgain[...] = dg
 
     rows = (ROW_LEN, D)
     return call(
-        body, "enc_ffn_back", [meta, du, h1, de, gains, *arrays], [SM, VM, VM, VM, VM] + [ANY] * n,
+        body, "enc_ffn_back", [meta, du, h1, de, gains, *arrays], [SM, ANY, ANY, ANY, VM] + [ANY] * n,
         [(rows, F32), (rows, BF), ((1, D), F32)], [VM, VM, VM],
-        [pltpu.VMEM((FF, D), BF), pltpu.VMEM(rows, F32), pltpu.SemaphoreType.DMA((4,))],
+        [pltpu.VMEM((FF, D), BF), pltpu.VMEM(rows, F32), pltpu.VMEM((BLOCKS, ROW_LEN, D), BF), pltpu.VMEM(rows, F32),
+         pltpu.VMEM(rows, BF), pltpu.SemaphoreType.DMA((10,))],
         us=8,
     )
 
@@ -572,13 +647,18 @@
     n = len(arrays)
     wide = 2 * TILE
 
-    def body(meta, da, q, k, v, lse, segr, segc, windows, *rest):
+    def body(meta, da, q_in, k_in, v_in, lse, segr, segc, windows, *rest):
         parts, rest = rest[:n], rest[n:]
-        dq, dk, dv, diag, other, w, dc, tiles, sums, kacc, vacc, sem = rest
+        dq_out, dk_out, dv_out, diag, other, w, dc, tiles, sums, kacc, vacc, q, k, v, dq, dk, dv, sems = rest
+        sem = sems.at[0]
         start_fetch(meta, parts, plan, [(0, GROUP, lambda core, g: GROUP * g)], w, sem, only=0)
+        for at, (src, dst) in enumerate(((q_in, q), (k_in, k), (v_in, v))):
+            start_copy(src, dst, sems.at[1 + at])
         fill_bias(windows, tiles, True)
         drain(w, sem)
         dc[...] = nt(da[...], w[...]).astype(BF)
+        for at, ref in enumerate((q, k, v)):
+            drain(ref, sems.at[1 + at])
         row = lax.broadcasted_iota(jnp.int32, (TILE, TILE), 0)
         col = lax.broadcasted_iota(jnp.int32, (TILE, TILE), 1)
         flip = (row + col == TILE - 1).astype(F32)
@@ -594,12 +674,7 @@
                     rows = slice(ib * wide, (ib + 1) * wide)
                     same = segc[...] == segr[:, rows]
                     qp, dcp = q[rows, cols], dc[rows, cols]
-                    bias = jnp.concatenate([
-                        jnp.concatenate([
-                            tiles[h, min(max(jb - (2 * ib + i), -2), 2) + 2] for i in range(2)
-                        ], axis=1) for jb in range(ROW_LEN // TILE)
-                    ], axis=0)
-                    s = jnp.where(same, nt(km, qp) + bias, MASKED)
+                    s = jnp.where(same, nt(km, qp) + bias_block(tiles, h, ib), MASKED)
                     prob = jnp.exp(s - lse[pl.ds(h, 1), rows])
                     dprob = nt(vm, dcp)
                     inner = jnp.sum(prob * dprob, axis=0, keepdims=True)
@@ -638,24 +713,28 @@
 
         lax.fori_loop(0, HEADS // 2, pair, 0)
 
-        @pl.when(meta[1] == 0)
-        def _():
-            other[0] = dk[...]
-            other[1] = dv[...]
-
-        @pl.when(meta[1] != 0)
-        def _():
-            other[0] = dq[...]
-            other[1] = da[...]
+        for core, (one, two) in enumerate(((dk, dv), (dq, da))):
+
+            @pl.when(meta[1] == core)
+            def _():
+                start_copy(one, other.at[0], sems.at[1])
+                start_copy(two, other.at[1], sems.at[1])
+
+        for src, dst in ((dq, dq_out), (dk, dk_out), (dv, dv_out)):
+            start_copy(src, dst, sems.at[2])
+        drain(dk, sems.at[1])
+        drain(dv, sems.at[1])
+        for ref in (dq, dk, dv):
+            drain(ref, sems.at[2])
 
     rows = (ROW_LEN, D)
     return call(
         body, "enc_attention_back", [meta, da, q, k, v, lse, segr, segc, windows, *arrays],
-        [SM] + [VM] * 8 + [ANY] * n,
-        [(rows, BF), (rows, BF), (rows, BF), ((HEADS, 5, 2 * TILE), F32), ((2,) + rows, BF)], [VM] * 5,
+        [SM, VM, ANY, ANY, ANY] + [VM] * 4 + [ANY] * n,
+        [(rows, BF), (rows, BF), (rows, BF), ((HEADS, 5, 2 * TILE), F32), ((2,) + rows, BF)], [ANY, ANY, ANY, VM, ANY],
         [pltpu.VMEM((D, D), BF), pltpu.VMEM(rows, BF), pltpu.VMEM((HEADS, 5, TILE, TILE), F32),
-         pltpu.VMEM((5, TILE, TILE), F32), pltpu.VMEM((ROW_LEN, TILE), F32), pltpu.VMEM((ROW_LEN, TILE), F32),
-         pltpu.SemaphoreType.DMA],
+         pltpu.VMEM((5, TILE, TILE), F32), pltpu.VMEM((ROW_LEN, TILE), F32), pltpu.VMEM((ROW_LEN, TILE), F32)]
+        + [pltpu.VMEM(rows, BF)] * 6 + [pltpu.SemaphoreType.DMA((4,))],
         us=25,
     )
 
@@ -691,13 +770,23 @@
 
     def body(meta, dq, dk, dv, x, dh1, gains, *rest):
         a_parts, b_parts, rest = rest[:n], rest[n : 2 * n], rest[2 * n :]
-        keep, send, dgain, w, sem = rest
-        start_fetch(meta, a_parts, a_plan, [(0, GROUP, lambda core, g: core * D + GROUP * g)], w, sem)
-        start_fetch(meta, b_parts, b_plan, [(0, GROUP, lambda core, g: 2 * D + GROUP * g)], w, sem, only=1)
-        drain(w, sem)
-        total = nt(dq[...], w[0:D, :]) + nt(dk[...], w[D : 2 * D, :]) + nt(dv[...], w[2 * D :, :])
-        dx, dg = rms_back(x[...].astype(F32), gains[0:1, :], total)
-        out = (dh1[...] + dx).astype(BF)
+        keep, send, dgain, w, grads, xs, dh1s, sems = rest
+        start_fetch(meta, a_parts, a_plan, [(0, GROUP, lambda core, g: core * D + GROUP * g, lambda core, g: core)], w, sems)
+        start_fetch(meta, b_parts, b_plan, [(0, GROUP, lambda core, g: 2 * D + GROUP * g, lambda core, g: 2)], w, sems, only=1)
+        for k, ref in enumerate((dq, dk, dv)):
+            start_copy(ref, grads.at[k], sems.at[3 + k])
+        start_copy(x, xs, sems.at[6])
+        start_copy(dh1, dh1s, sems.at[7])
+        total = None
+        for k in range(3):
+            drain(w.at[pl.ds(k * D, D)], sems.at[k])
+            drain(grads.at[k], sems.at[3 + k])
+            part = nt(grads[k], w[k * D : (k + 1) * D, :])
+            total = part if total is None else total + part
+        drain(xs, sems.at[6])
+        drain(dh1s, sems.at[7])
+        dx, dg = rms_back(xs[...].astype(F32), gains[0:1, :], total)
+        out = (dh1s[...] + dx).astype(BF)
         dgain[...] = dg
         half = D // 2
 
@@ -713,9 +802,10 @@
 
     return call(
         body, "enc_input_grad", [meta, dq, dk, dv, x, dh1, gains, *a_arrays, *b_arrays],
-        [SM] + [VM] * 6 + [ANY] * (2 * n),
+        [SM] + [ANY] * 5 + [VM] + [ANY] * (2 * n),
         [((ROW_LEN, D // 2), BF), ((ROW_LEN, D // 2), BF), ((1, D), F32)], [VM] * 3,
-        [pltpu.VMEM((3 * D, D), BF), pltpu.SemaphoreType.DMA],
+        [pltpu.VMEM((3 * D, D), BF), pltpu.VMEM((3, ROW_LEN, D), BF), pltpu.VMEM((ROW_LEN, D), BF),
+         pltpu.VMEM((ROW_LEN, D), F32), pltpu.SemaphoreType.DMA((8,))],
         us=1,
     )
 
@@ -933,7 +1023,7 @@
         body, "dec_weight_grads", [place, own, got, g_all, w_back], [SM, VM, VM, VM, VM],
         [((rows, D), F32), ((rows, D), F32), ((rows, FF), F32), ((4 * rows, D), F32), ((self_rows, D), F32),
          ((self_rows, D), F32), (g_all.shape, BF)], [VM] * 7,
-        [], us=5,
+        [], us=0.2,
     )
 
 
@@ -1096,7 +1186,6 @@
     keep, send, dg_attn0 = enc_input_grad(meta, dq, dk, dv, x, dh1, gains0, sa.sets(sa_got), sb.sets(sb_got))
     got, dq, dg_attn0 = phase(backs, got, dq, dg_attn0)
     backs.step(Z1)
-    square_a, square_b = two(enc_square_grads(meta, n1, n1_got, c, c_got, dq, dk, dv, da, got))
     table = jnp.einsum("hdt,dtb->bh", diag, diagonal_onehots(), precision=lax.Precision.HIGHEST)
     little = jnp.concatenate([
         dg_attn0, dg_ffn0, dg_attn1, dg_ffn1, dg_self,
@@ -1105,10 +1194,13 @@
     little = little + across(little)
     for bit in range(pre):
         little = little + along(little, bit)
-    acts, little = phase(square_a, square_b, in_a, in_b, acts, little)
+    other = along(little, Z0 + pre)
+    square_a, square_b = two(enc_square_grads(meta, n1, n1_got, c, c_got, dq, dk, dv, da, got))
+    acts, other = phase(square_a, square_b, in_a, in_b, acts, other)
+    little = little + other
     square_a.step(Y), square_b.step(X)
     theirs = across(acts)
-    other = along(little, X + pre)
+    other = along(little, Z1 + pre)
     ins = merged([in_a, in_b])
     ins.step(Z0)
 
@@ -1118,18 +1210,17 @@
     other, y = phase(square_a, square_b, ins, backs, other, y)
     little = little + other
     square_a.step(X), square_b.step(Y), ins.step(Z1)
-    other = along(little, Y + pre)
-    other, y, send, z2 = phase(square_a, square_b, other, y, send, z2)
+    other = along(little, X + pre)
+    other, y, send, z2, dec_grad = phase(square_a, square_b, other, y, send, z2, dec_grad)
     little = little + other
     squares = merged([square_a, square_b])
     squares.step(Z0)
-    other = along(little, Z0 + pre)
+    other = along(little, Y + pre)
     z2 = z2 + across(z2)
     y = lax.all_to_all(y.reshape(chips, 8, D), "dp", 0, 0)
     other, y = phase(squares, ins, other, y)
     little = little + other
     squares.step(Z1)
-    little = little + along(little, Z1 + pre)
     backs_sum, ins_sum, square_sum = backs.total(), ins.total(), squares.total()
     dec_out = (z2 + jnp.sum(y.astype(F32), axis=0)).astype(BF)
     dec_out = jnp.where(first, across(dec_out), dec_out)

time: 377 us -> 370 us (0.981)
  Pallas kernels: 138 us -> 131 us
    pallas_call x14, Pallas kernels: 138 us -> 131 us  [call(): pl.pallas_call(body, name=name, out_shape=[jax.ShapeDtypeStruct(s, k) for...]
    unnamed x130 -> x148, local copies, waits for them, and re-layouts: 7.29 us -> 8.87 us
  transfers between devices with their start and end apart: 73 -> 73, of which waited for: 24 -> 27; matrix products, arithmetic and copies ran while one was open for 8% -> 8% of each run, Pallas kernels for 35% -> 34%
where the time goes in v1:
time: 370 us; the launch traced here: 363 us
  Pallas kernels  131 us (35%)
  waiting for transfers between devices  91.7 us (25%)
  starting transfers between devices  62.7 us (17%)
  local copies, waits for them, and re-layouts  23.4 us (6%)
  blocking collectives  20.3 us (5%)
  other arithmetic  16.7 us (5%)
  between operations  16.1 us (4%)
    pallas_call x14, Pallas kernels, call(): pl.pallas_call(body, name=name, out_shape=[jax.ShapeDtypeStruct(s, k) for...  131 us
    ppermute x38, waiting for transfers between devices, along(): return lax.ppermute(value, 'dp', [(i, i ^ 1 << bit) for i in range(count)])  78.6 us
    ppermute x38, starting transfers between devices, along(): return lax.ppermute(value, 'dp', [(i, i ^ 1 << bit) for i in range(count)])  51.2 us
    all_to_all x1, blocking collectives, per_device(): gw = lax.all_to_all(gw, 'dp', 0, 0)  20.3 us
    ppermute x32, waiting for transfers between devices, across(): return lax.ppermute(value, 'section', [(0, 1), (1, 0)])  10.6 us
    unnamed x148, local copies, waits for them, and re-layouts  8.87 us
  transfers between devices with their start and end apart: 73, of which 27 were waited for; matrix products, arithmetic and copies ran while one was open for 8% of the time, Pallas kernels for 34%

profile of v1, /device:TPU:0, one launch (start us, length us, event | category | flops | bytes accessed | tf_op | source)
XLA Modules:
  0.0 362.9 jit_solution(17189586893278373139)
XLA Ops:
  7.9 2.2 prepare.1
  14.9 3.3 collective-permute-start.2
  19.4 2.7 collective-permute-start.1
  24.9 3.2 collective-permute-done.1
  28.2 3.2 collective-permute-start.3
  32.2 3.3 collective-permute-done.4
  35.5 9.0 %collective-permute-done.3 = bf16[2,96,768]{2,1,0:T(8,128)(2,1)S(1)} collective-permute-done((bf16[2,96,768]{2,1,0:T(8,128)(2,1)S(1)}, bf16[2,96,768]{2,1,0:T(8,128)(2,1)S(1)}, u32[]{:S(2)}, u32[]{:S(2)}) %collective-permute-start.3) | collective-permute-done | bytes 294944 | tf_op jit(solution)/shard_map/ppermute | solution.py:68
  46.9 1.8 collective-permute-start.7
  48.7 1.8 collective-permute-start.8
  50.5 9.9 %collective-permute-done.8 = bf16[4,16,768]{2,1,0:T(8,128)(2,1)S(1)} collective-permute-done((bf16[4,16,768]{2,1,0:T(8,128)(2,1)S(1)}, bf16[4,16,768]{2,1,0:T(8,128)(2,1)S(1)}, u32[]{:S(2)}, u32[]{:S(2)}) %collective-permute-start.8) | collective-permute-done | bytes 98336 | tf_op jit(solution)/shard_map/ppermute | solution.py:68
  60.4 9.6 %collective-permute-done.7 = bf16[1,144,768]{2,1,0:T(8,128)(2,1)S(1)} collective-permute-done((bf16[1,144,768]{2,1,0:T(8,128)(2,1)S(1)}, bf16[1,144,768]{2,1,0:T(8,128)(2,1)S(1)}, u32[]{:S(2)}, u32[]{:S(2)}) %collective-permute-start.7) | collective-permute-done | bytes 221216 | tf_op jit(solution)/shard_map/ppermute | solution.py:68
  71.4 3.2 collective-permute-start.12
  74.6 13.9 %collective-permute-done.12 = bf16[8,16,768]{2,1,0:T(8,128)(2,1)S(1)} collective-permute-done((bf16[8,16,768]{2,1,0:T(8,128)(2,1)S(1)}, bf16[8,16,768]{2,1,0:T(8,128)(2,1)S(1)}, u32[]{:S(2)}, u32[]{:S(2)}) %collective-permute-start.12) | collective-permute-done | bytes 196640 | tf_op jit(solution)/shard_map/ppermute | solution.py:68
  88.5 2.3 collective-permute-done.11
  91.8 2.0 collective-permute-done.15
  97.8 17.0 %enc_attention.1 = (bf16[512,768]{1,0:T(8,128)(2,1)}, bf16[512,768]{1,0:T(8,128)(2,1)}, bf16[512,768]{1,0:T(8,128)(2,1)}, bf16[512,768]{1,0:T(8,128)(2,1)}, bf16...) custom-call(s32[2]{0:T(128)} %pad_add_fusion.meta, ...), custom_call_target="tpu_custom_call" | custom-call | flops 5500000256 | bytes 5000000 | tf_op jit(solution)/shard_map/enc_attention/pallas_call | solution.py:353
  114.8 5.1 %collective-permute-done.13 = bf16[4,80,768]{2,1,0:T(8,128)(2,1)S(1)} collective-permute-done((bf16[4,80,768]{2,1,0:T(8,128)(2,1)S(1)}, bf16[4,80,768]{2,1,0:T(8,128)(2,1)S(1)}, u32[]{:S(2)}, u32[]{:S(2)}) %collective-permute-start.13) | collective-permute-done | bytes 491552 | tf_op jit(solution)/shard_map/ppermute | solution.py:68
  126.2 20.3 %all_to_all.10 = bf16[16,8,256]{2,1,0:T(8,128)(2,1)S(1)} all-to-all(bf16[16,8,256]{2,1,0:T(8,128)(2,1)S(1)} %pad_bitcast_fusion), channel_id=1, replica_groups=mesh['section'=2,'dp'=16] {'dp'}, dimensions={0} | all-to-all | bytes 131072 | tf_op jit(solution)/shard_map/all_to_all | solution.py:1122
  146.5 2.6 slice.323
  151.6 2.2 collective-permute-done.24.rest_6_.rest_10_.rest_2_
  154.3 1.6 collective-permute-done.20.rest_2_
  158.6 15.1 %enc_ffn.1 = (bf16[512,3072]{1,0:T(8,128)(2,1)}, bf16[512,3072]{1,0:T(8,128)(2,1)}, bf16[512,768]{1,0:T(8,128)(2,1)}) custom-call(s32[2]{0:T(128)} %pad_add_fusion.meta, f32[512,768]{1,0:T(8,128)} %get-tuple-element.338.h1, bf16[512,768]{1,0:T(8,128)(2,1)} %get-tuple-element.330.n2, bf16[8,80,768]{2,1,0:T(8,128)(2,1)} %constant_dynamic-update-slice_fusion.16.rest_0_, ...), custom_call_target="tpu_custom_call" | custom-call | flops 4124999936 | bytes 3750000 | tf_op jit(solution)/shard_map/enc_ffn/pallas_call | solution.py:353
  175.2 5.1 %dec_before.1 = (bf16[8,768]{1,0:T(8,128)(2,1)}, bf16[8,768]{1,0:T(8,128)(2,1)}, f32[8,768]{1,0:T(8,128)}, bf16[8,768]{1,0:T(8,128)(2,1)}, bf16[8,768]{1,0:T(8,1...) custom-call(s32[2]{0:T(128)} %pad_add_fusion.meta, bf16[8,768]{1,0:T(8,128)(2,1)} %z.3, bf16[8,768]{1,0:T(8,128)(2,1)} %d_out.1, ...), custom_call_target="tpu_custom_call" | custom-call | flops 1650000000 | bytes 1500000 | tf_op jit(solution)/shard_map/dec_before/pallas_call | solution.py:353
  181.3 9.6 %dec_core.1 = (bf16[512,768]{1,0:T(8,128)(2,1)}, bf16[8,768]{1,0:T(8,128)(2,1)}, f32[8,768]{1,0:T(8,128)}, bf16[8,768]{1,0:T(8,128)(2,1)}, bf16[8,3072]{1,0:T(8,...) custom-call(s32[2]{0:T(128)} %pad_add_fusion.meta, ...), custom_call_target="tpu_custom_call" | custom-call | flops 2750000128 | bytes 2500000 | tf_op jit(solution)/shard_map/dec_core/pallas_call | solution.py:353
  191.5 9.2 %enc_hidden_grad.1 = (bf16[512,3072]{1,0:T(8,128)(2,1)}, bf16[512,1536]{1,0:T(8,128)(2,1)}) custom-call(s32[2]{0:T(128)} %pad_add_fusion.meta, bf16[512,768]{1,0:T(8,128)(2,1)} %get-tuple-element.293.de, bf16[512,3072]{1,0:T(8,128)(2,1)} %get-tuple-element.296.slope, bf16[8,64,768]{2,1,0:T(8,128)(2,1)} %copy-done.2, bf16[8,64,768]{2,1,0:T(8,128)(2,1)} %copy-done.3, ...), custom_call_target="tpu_custom_call" | custom-call | flops 2200000000 | bytes 2000000 | tf_op jit(solution)/shard_map/enc_hidden_grad/pallas_call | solution.py:353
  201.4 6.0 %dec_after.1 = (bf16[8,6528]{1,0:T(8,128)(2,1)}, bf16[8,6528]{1,0:T(8,128)(2,1)}, bf16[8,768]{1,0:T(8,128)(2,1)}, f32[1,768]{1,0:T(1,128)}, f32[1,768]{1,0:T(1,1...) custom-call(s32[2]{0:T(128)} %pad_add_fusion.meta, bf16[8,768]{1,0:T(8,128)(2,1)} %z.3, ...), custom_call_target="tpu_custom_call" | custom-call | flops 1650000000 | bytes 1500000 | tf_op jit(solution)/shard_map/dec_after/pallas_call | solution.py:353
  209.1 7.4 %enc_w_back_grad.1 = (bf16[8,48,768]{2,1,0:T(8,128)(2,1)}, bf16[8,48,768]{2,1,0:T(8,128)(2,1)}, bf16[8,48,768]{2,1,0:T(8,128)(2,1)}, bf16[8,48,768]{2,1,0:T(8,128)(2,1)}) custom-call(s32[2]{0:T(128)} %pad_add_fusion.meta, bf16[512,768]{1,0:T(8,128)(2,1)} %get-tuple-element.293.de, bf16[512,384]{1,0:T(8,128)(2,1)} %copy-done.34, ...), custom_call_target="tpu_custom_call" | custom-call | flops 1924999936 | bytes 1750000 | tf_op jit(solution)/shard_map/enc_w_back_grad/pallas_call | solution.py:353
  216.5 1.9 collective-permute-start.37
  219.3 6.6 %enc_w_in_grad.1 = (bf16[8,96,768]{2,1,0:T(8,128)(2,1)}, bf16[8,96,768]{2,1,0:T(8,128)(2,1)}, bf16[8,48,768]{2,1,0:T(8,128)(2,1)}, bf16[8,48,768]{2,1,0:T(8,128)(2,1)}) custom-call(s32[2]{0:T(128)} %pad_add_fusion.meta, bf16[512,3072]{1,0:T(8,128)(2,1)} %get-tuple-element.328.du, ...), custom_call_target="tpu_custom_call", output_to_operand_aliasing={{0}: (5, {}), {1}: (6, {})} | custom-call | flops 1924999936 | bytes 1750000 | tf_op jit(solution)/shard_map/enc_w_in_grad/pallas_call | solution.py:353
  227.5 9.0 %enc_ffn_back.1 = (f32[512,768]{1,0:T(8,128)}, bf16[512,768]{1,0:T(8,128)(2,1)}, f32[1,768]{1,0:T(1,128)}) custom-call(s32[2]{0:T(128)} %pad_add_fusion.meta, bf16[512,3072]{1,0:T(8,128)(2,1)} %get-tuple-element.328.du, f32[512,768]{1,0:T(8,128)} %get-tuple-element.338.h1, bf16[512,768]{1,0:T(8,128)(2,1)} %get-tuple-element.293.de, ...), custom_call_target="tpu_custom_call" | custom-call | flops 2200000000 | bytes 2000000 | tf_op jit(solution)/shard_map/enc_ffn_back/pallas_call | solution.py:353
  237.3 1.9 collective-permute-start.40
  239.5 23.9 %enc_attention_back.1 = (bf16[512,768]{1,0:T(8,128)(2,1)}, bf16[512,768]{1,0:T(8,128)(2,1)}, bf16[512,768]{1,0:T(8,128)(2,1)}, f32[12,5,256]{2,1,0:T(8,128)}, bf16[2,512,768]{2,1,0:T(8,128)(2,1)}) custom-call(s32[2]{0:T(128)} %pad_add_fusion.meta, bf16[512,768]{1,0:T(8,128)(2,1)} %get-tuple-element.348.da, bf16[512,768]{1,0:T(8,128)(2,1)} %get-tuple-element.349.q_in, ...), custom_call_target="tpu_custom_call" | custom-call | flops 6874999808 | bytes 6250000 | tf_op jit(solution)/shard_map/enc_attention_back/pallas_call | solution.py:353
  263.4 3.7 %collective-permute-done.40 = bf16[4,48,768]{2,1,0:T(8,128)(2,1)S(1)} collective-permute-done((bf16[4,48,768]{2,1,0:T(8,128)(2,1)S(1)}, bf16[4,48,768]{2,1,0:T(8,128)(2,1)S(1)}, u32[]{:S(2)}, u32[]{:S(2)}) %collective-permute-start.40) | collective-permute-done | bytes 294944 | tf_op jit(solution)/shard_map/ppermute | solution.py:68
  274.8 7.8 %enc_input_grad.1 = (bf16[512,384]{1,0:T(8,128)(2,1)}, bf16[512,384]{1,0:T(8,128)(2,1)}, f32[1,768]{1,0:T(1,128)}) custom-call(s32[2]{0:T(128)} %pad_add_fusion.meta, bf16[512,768]{1,0:T(8,128)(2,1)} %get-tuple-element.365.dq, bf16[512,768]{1,0:T(8,128)(2,1)} %get-tuple-element.361.dk, bf16[512,768]{1,0:T(8,128)(2,1)} %get-tuple-element.362.dv, ...), custom_call_target="tpu_custom_call" | custom-call | flops 275000000 | bytes 250000 | tf_op jit(solution)/shard_map/enc_input_grad/pallas_call | solution.py:353
  286.7 7.1 %enc_square_grads.1 = (bf16[8,48,768]{2,1,0:T(8,128)(2,1)}, bf16[8,48,768]{2,1,0:T(8,128)(2,1)}, bf16[8,48,768]{2,1,0:T(8,128)(2,1)}, bf16[8,48,768]{2,1,0:T(8,128)(2,1)}) custom-call(s32[2]{0:T(128)} %pad_add_fusion.meta, bf16[512,768]{1,0:T(8,128)(2,1)} %get-tuple-element.266.n1, bf16[512,768]{1,0:T(8,128)(2,1)} %copy-done.17, ...), custom_call_target="tpu_custom_call" | custom-call | flops 275000000 | bytes 250000 | tf_op jit(solution)/shard_map/enc_square_grads/pallas_call | solution.py:353
  294.8 2.0 collective-permute-start.50
  300.0 1.8 collective-permute-start.52
  302.8 2.2 collective-permute-start.54
  305.8 5.5 %dec_weight_grads.1 = (f32[48,768]{1,0:T(8,128)}, f32[48,768]{1,0:T(8,128)}, f32[48,3072]{1,0:T(8,128)}, f32[192,768]{1,0:T(8,128)}, f32[24,768]{1,0:T(8,128)}, ...) custom-call(s32[2]{0:T(128)} %pad_add_fusion.1.place, bf16[128,6528]{1,0:T(8,128)(2,1)} %all-gather.7.cloned.1.call-done.own, ...), custom_call_target="tpu_custom_call" | custom-call | flops 55000000 | bytes 50000 | tf_op jit(solution)/shard_map/dec_weight_grads/pallas_call | solution.py:353
  311.3 3.4 collective-permute-done.53
  319.6 2.5 collective-permute-start.61
  322.1 4.4 %collective-permute-done.57 = bf16[4,48,768]{2,1,0:T(8,128)(2,1)S(1)} collective-permute-done((bf16[4,48,768]{2,1,0:T(8,128)(2,1)S(1)}, bf16[4,48,768]{2,1,0:T(8,128)(2,1)S(1)}, u32[]{:S(2)}, u32[]{:S(2)}) %collective-permute-start.57) | collective-permute-done | bytes 294944 | tf_op jit(solution)/shard_map/ppermute | solution.py:68
  327.0 2.2 collective-permute-start.60
  329.2 4.7 %all-to-all-start.1 = ((bf16[16,8,768]{2,1,0:T(8,128)(2,1)}), bf16[16,8,768]{2,1,0:T(8,128)(2,1)S(1)}, u32[]{:S(2)}, u32[]{:S(2)}) async-start(bf16[16,8,768]{2,1,0:T(8,128)(2,1)} %bitcast.116), calls=%async_computation.1 | async-start | bytes 393216 | tf_op jit(solution)/shard_map/all_to_all | solution.py:1220
  335.0 2.0 collective-permute-start.62
  339.1 1.9 collective-permute-done.60
  341.0 2.4 all-to-all-done.1
  347.9 5.0 %collective-permute-done.66 = bf16[1,96,768]{2,1,0:T(8,128)(2,1)S(1)} collective-permute-done((bf16[1,96,768]{2,1,0:T(8,128)(2,1)S(1)}, bf16[1,96,768]{2,1,0:T(8,128)(2,1)S(1)}, u32[]{:S(2)}, u32[]{:S(2)}) %collective-permute-start.66) | collective-permute-done | bytes 147488 | tf_op jit(solution)/shard_map/ppermute | solution.py:68
  (382 shorter events, 72.7 us)
Async XLA Ops:
  7.2 139.3 %all-gather.5.cloned.1.call-start = ((), (), s32[]{:S(2)}) async-start(), calls=%async_computation.2 | async-start | bytes 7520256 | tf_op jit(solution)/shard_map/all_gather | solution.py:1069
  14.3 279.5 %all-gather.7.cloned.1.call-start = ((), (), s32[]{:S(2)}) async-start(), calls=%async_computation.3 | async-start | bytes 1775616 | tf_op jit(solution)/shard_map/all_gather | solution.py:1170
  14.9 10.0 %collective-permute-start.2 = (bf16[1,16,768]{2,1,0:T(8,128)(2,1)S(1)}, bf16[1,16,768]{2,1,0:T(8,128)(2,1)S(1)}, u32[]{:S(2)}, u32[]{:S(2)}) collective-permute-start(bf16[1,16,768]{2,1,0:T(8,128)(2,1)S(1)} %maximum_bitcast_fusion.1), channel_id=1, source_target_pairs={{0,1},{1,0},{2,3},{3,2},{4,5},{5,4},{6,7},{7,6},{8,9},{9,8},{10,11... | collective-permute-start | bytes 73736 | tf_op jit(solution)/shard_map/ppermute | solution.py:68
  28.2 16.3 %collective-permute-start.3 = (bf16[2,96,768]{2,1,0:T(8,128)(2,1)S(1)}, bf16[2,96,768]{2,1,0:T(8,128)(2,1)S(1)}, u32[]{:S(2)}, u32[]{:S(2)}) collective-permute-start(bf16[2,96,768]{2,1,0:T(8,128)(2,1)S(1)} %constant_dynamic-update-slice_fusion), channel_id=1, source_target_pairs={{0,4},{1,5},{2,6},{3,7},{4,0},{5,1},{6,2},{7,3},{8,12},{9,13},{10,... | collective-permute-start | bytes 884744 | tf_op jit(solution)/shard_map/ppermute | solution.py:68
  44.6 25.4 %collective-permute-start.6 = (bf16[4,48,768]{2,1,0:T(8,128)(2,1)S(1)}, bf16[4,48,768]{2,1,0:T(8,128)(2,1)S(1)}, u32[]{:S(2)}, u32[]{:S(2)}) collective-permute-start(bf16[4,48,768]{2,1,0:T(8,128)(2,1)S(1)} %pad_maximum_fusion.5), channel_id=1, source_target_pairs={{0,2},{1,3},{2,0},{3,1},{4,6},{5,7},{6,4},{7,5},{8,10},{9,11},{10,... | collective-permute-start | bytes 884744 | tf_op jit(solution)/shard_map/ppermute | solution.py:68
  46.2 23.9 %collective-permute-start.5 = (bf16[4,48,768]{2,1,0:T(8,128)(2,1)S(1)}, bf16[4,48,768]{2,1,0:T(8,128)(2,1)S(1)}, u32[]{:S(2)}, u32[]{:S(2)}) collective-permute-start(bf16[4,48,768]{2,1,0:T(8,128)(2,1)S(1)} %pad_maximum_fusion.4), channel_id=1, source_target_pairs={{0,1},{1,0},{2,3},{3,2},{4,5},{5,4},{6,7},{7,6},{8,9},{9,8},{10,11... | collective-permute-start | bytes 884744 | tf_op jit(solution)/shard_map/ppermute | solution.py:68
  46.9 23.1 %collective-permute-start.7 = (bf16[1,144,768]{2,1,0:T(8,128)(2,1)S(1)}, bf16[1,144,768]{2,1,0:T(8,128)(2,1)S(1)}, u32[]{:S(2)}, u32[]{:S(2)}) collective-permute-start(bf16[1,144,768]{2,1,0:T(8,128)(2,1)S(1)} %maximum_bitcast_fusion), channel_id=1, source_target_pairs={{0,8},{1,9},{2,10},{3,11},{4,12},{5,13},{6,14},{7,15},{8,0},{9,1},... | collective-permute-start | bytes 663560 | tf_op jit(solution)/shard_map/ppermute | solution.py:68
  48.7 11.7 %collective-permute-start.8 = (bf16[4,16,768]{2,1,0:T(8,128)(2,1)S(1)}, bf16[4,16,768]{2,1,0:T(8,128)(2,1)S(1)}, u32[]{:S(2)}, u32[]{:S(2)}) collective-permute-start(bf16[4,16,768]{2,1,0:T(8,128)(2,1)S(1)} %constant_dynamic-update-slice_fusion.4), channel_id=1, source_target_pairs={{0,4},{1,5},{2,6},{3,7},{4,0},{5,1},{6,2},{7,3},{8,12},{9,13},{10,... | collective-permute-start | bytes 294920 | tf_op jit(solution)/shard_map/ppermute | solution.py:68
  70.1 20.7 %collective-permute-start.10 = (bf16[8,48,768]{2,1,0:T(8,128)(2,1)S(1)}, bf16[8,48,768]{2,1,0:T(8,128)(2,1)S(1)}, u32[]{:S(2)}, u32[]{:S(2)}) collective-permute-start(bf16[8,48,768]{2,1,0:T(8,128)(2,1)S(1)} %constant_dynamic-update-slice_fusion.8.rest_4_.rest_0_), channel_id=1, source_target_pairs={{0,1},{1,0},{2,3},{3,2},{4,5},{5,4},{6,7},{7,6},{8,9},{9,8},{10,11... | collective-permute-start | bytes 1769480 | tf_op jit(solution)/shard_map/ppermute | solution.py:68
  71.2 19.6 %collective-permute-start.9 = (bf16[8,48,768]{2,1,0:T(8,128)(2,1)S(1)}, bf16[8,48,768]{2,1,0:T(8,128)(2,1)S(1)}, u32[]{:S(2)}, u32[]{:S(2)}) collective-permute-start(bf16[8,48,768]{2,1,0:T(8,128)(2,1)S(1)} %constant_dynamic-update-slice_fusion.6.rest_0_), channel_id=1, source_target_pairs={{0,2},{1,3},{2,0},{3,1},{4,6},{5,7},{6,4},{7,5},{8,10},{9,11},{10,... | collective-permute-start | bytes 1769480 | tf_op jit(solution)/shard_map/ppermute | solution.py:68
  71.3 19.5 %collective-permute-start.11 = (bf16[2,144,768]{2,1,0:T(8,128)(2,1)S(1)}, bf16[2,144,768]{2,1,0:T(8,128)(2,1)S(1)}, u32[]{:S(2)}, u32[]{:S(2)}) collective-permute-start(bf16[2,144,768]{2,1,0:T(8,128)(2,1)S(1)} %constant_dynamic-update-slice_fusion.10), channel_id=1, source_target_pairs={{0,4},{1,5},{2,6},{3,7},{4,0},{5,1},{6,2},{7,3},{8,12},{9,13},{10,... | collective-permute-start | bytes 1327112 | tf_op jit(solution)/shard_map/ppermute | solution.py:68
  71.4 17.1 %collective-permute-start.12 = (bf16[8,16,768]{2,1,0:T(8,128)(2,1)S(1)}, bf16[8,16,768]{2,1,0:T(8,128)(2,1)S(1)}, u32[]{:S(2)}, u32[]{:S(2)}) collective-permute-start(bf16[8,16,768]{2,1,0:T(8,128)(2,1)S(1)} %constant_dynamic-update-slice_fusion.12), channel_id=1, source_target_pairs={{0,8},{1,9},{2,10},{3,11},{4,12},{5,13},{6,14},{7,15},{8,0},{9,1},... | collective-permute-start | bytes 589832 | tf_op jit(solution)/shard_map/ppermute | solution.py:68
  74.6 21.1 %collective-permute-start.18 = (bf16[8,48,768]{2,1,0:T(8,128)(2,1)S(1)}, bf16[8,48,768]{2,1,0:T(8,128)(2,1)S(1)}, u32[]{:S(2)}, u32[]{:S(2)}) collective-permute-start(bf16[8,48,768]{2,1,0:T(8,128)(2,1)S(1)} %constant_dynamic-update-slice_fusion.8.rest_4_.rest_0_), channel_id=1, source_target_pairs={{0,16},{16,0},{1,17},{17,1},{2,18},{18,2},{3,19},{19,3},{4,20},{20... | collective-permute-start | bytes 1769480 | tf_op jit(solution)/shard_map/ppermute | solution.py:63
  93.9 20.9 %collective-permute-start.14 = (bf16[4,64,768]{2,1,0:T(8,128)(2,1)S(1)}, bf16[4,64,768]{2,1,0:T(8,128)(2,1)}, u32[]{:S(2)}, u32[]{:S(2)}) collective-permute-start(bf16[4,64,768]{2,1,0:T(8,128)(2,1)S(1)} %pad_maximum_fusion.3), channel_id=1, source_target_pairs={{0,2},{1,3},{2,0},{3,1},{4,6},{5,7},{6,4},{7,5},{8,10},{9,11},{10,... | collective-permute-start | bytes 1179656 | tf_op jit(solution)/shard_map/ppermute | solution.py:68
  95.7 24.2 %collective-permute-start.13 = (bf16[4,80,768]{2,1,0:T(8,128)(2,1)S(1)}, bf16[4,80,768]{2,1,0:T(8,128)(2,1)S(1)}, u32[]{:S(2)}, u32[]{:S(2)}) collective-permute-start(bf16[4,80,768]{2,1,0:T(8,128)(2,1)S(1)} %pad_maximum_fusion.1), channel_id=1, source_target_pairs={{0,1},{1,0},{2,3},{3,2},{4,5},{5,4},{6,7},{7,6},{8,9},{9,8},{10,11... | collective-permute-start | bytes 1474568 | tf_op jit(solution)/shard_map/ppermute | solution.py:68
  121.5 24.9 %collective-permute-start.21 = (bf16[8,80,768]{2,1,0:T(8,128)(2,1)}, bf16[8,80,768]{2,1,0:T(8,128)(2,1)}, u32[]{:S(2)}, u32[]{:S(2)}) collective-permute-start(bf16[8,80,768]{2,1,0:T(8,128)(2,1)} %constant_dynamic-update-slice_fusion.16.rest_0_), channel_id=1, source_target_pairs={{0,2},{1,3},{2,0},{3,1},{4,6},{5,7},{6,4},{7,5},{8,10},{9,11},{10,... | collective-permute-start | bytes 2949128 | tf_op jit(solution)/shard_map/ppermute | solution.py:68
  123.5 23.0 %collective-permute-start.22 = (bf16[8,64,768]{2,1,0:T(8,128)(2,1)S(1)}, bf16[8,64,768]{2,1,0:T(8,128)(2,1)S(1)}, u32[]{:S(2)}, u32[]{:S(2)}) collective-permute-start(bf16[8,64,768]{2,1,0:T(8,128)(2,1)S(1)} %constant_dynamic-update-slice_fusion.18.rest_4_.rest_8_.rest_0_), channel_id=1, source_target_pairs={{0,1},{1,0},{2,3},{3,2},{4,5},{5,4},{6,7},{7,6},{8,9},{9,8},{10,11... | collective-permute-start | bytes 2359304 | tf_op jit(solution)/shard_map/ppermute | solution.py:68
  157.4 16.7 %collective-permute-start.28 = (bf16[16,288,768]{2,1,0:T(8,128)(2,1)}, bf16[16,288,768]{2,1,0:T(8,128)(2,1)}, u32[]{:S(2)}, u32[]{:S(2)}) collective-permute-start(bf16[16,288,768]{2,1,0:T(8,128)(2,1)} %bitcast.103), channel_id=1, source_target_pairs={{0,16},{16,0},{1,17},{17,1},{2,18},{18,2},{3,19},{19,3},{4,20},{20... | collective-permute-start | bytes 21233672 | tf_op jit(solution)/shard_map/ppermute | solution.py:63
  157.6 16.6 %collective-permute-start.32 = (bf16[384,1536]{1,0:T(8,128)(2,1)S(1)}, bf16[384,1536]{1,0:T(8,128)(2,1)S(1)}, u32[]{:S(2)}, u32[]{:S(2)}) collective-permute-start(bf16[384,1536]{1,0:T(8,128)(2,1)S(1)} %pad_maximum_fusion.self_own.rest_8_), channel_id=1, source_target_pairs={{0,16},{16,0},{1,17},{17,1},{2,18},{18,2},{3,19},{19,3},{4,20},{20... | collective-permute-start | bytes 3538952 | tf_op jit(solution)/shard_map/ppermute | solution.py:63
  158.0 15.7 %collective-permute-start.29 = (bf16[512,768]{1,0:T(8,128)(2,1)}, bf16[512,768]{1,0:T(8,128)(2,1)S(1)}, u32[]{:S(2)}, u32[]{:S(2)}) collective-permute-start(bf16[512,768]{1,0:T(8,128)(2,1)} %get-tuple-element.266.n1), channel_id=1, source_target_pairs={{0,16},{16,0},{1,17},{17,1},{2,18},{18,2},{3,19},{19,3},{4,20},{20... | collective-permute-start | bytes 2359304 | tf_op jit(solution)/shard_map/ppermute | solution.py:63
  158.1 16.0 %collective-permute-start.30 = (bf16[512,768]{1,0:T(8,128)(2,1)}, bf16[512,768]{1,0:T(8,128)(2,1)}, u32[]{:S(2)}, u32[]{:S(2)}) collective-permute-start(bf16[512,768]{1,0:T(8,128)(2,1)} %get-tuple-element.278.c), channel_id=1, source_target_pairs={{0,16},{16,0},{1,17},{17,1},{2,18},{18,2},{3,19},{19,3},{4,20},{20... | collective-permute-start | bytes 2359304 | tf_op jit(solution)/shard_map/ppermute | solution.py:63
  158.5 15.7 %collective-permute-start.31 = (bf16[512,768]{1,0:T(8,128)(2,1)}, bf16[512,768]{1,0:T(8,128)(2,1)S(1)}, u32[]{:S(2)}, u32[]{:S(2)}) collective-permute-start(bf16[512,768]{1,0:T(8,128)(2,1)} %get-tuple-element.330.n2), channel_id=1, source_target_pairs={{0,16},{16,0},{1,17},{17,1},{2,18},{18,2},{3,19},{19,3},{4,20},{20... | collective-permute-start | bytes 2359304 | tf_op jit(solution)/shard_map/ppermute | solution.py:63
  180.4 27.0 %collective-permute-start.35 = (bf16[512,3072]{1,0:T(8,128)(2,1)}, bf16[512,3072]{1,0:T(8,128)(2,1)S(1)}, u32[]{:S(2)}, u32[]{:S(2)}) collective-permute-start(bf16[512,3072]{1,0:T(8,128)(2,1)} %get-tuple-element.317.f), channel_id=1, source_target_pairs={{0,16},{16,0},{1,17},{17,1},{2,18},{18,2},{3,19},{19,3},{4,20},{20... | collective-permute-start | bytes 9437192 | tf_op jit(solution)/shard_map/ppermute | solution.py:63
  190.9 9.8 %collective-permute-start.33 = (bf16[512,384]{1,0:T(8,128)(2,1)}, bf16[512,384]{1,0:T(8,128)(2,1)S(1)}, u32[]{:S(2)}, u32[]{:S(2)}) collective-permute-start(bf16[512,384]{1,0:T(8,128)(2,1)} %get-tuple-element.294), channel_id=1, source_target_pairs={{0,16},{16,0},{1,17},{17,1},{2,18},{18,2},{3,19},{19,3},{4,20},{20... | collective-permute-start | bytes 1179656 | tf_op jit(solution)/shard_map/ppermute | solution.py:63
  191.4 9.3 %collective-permute-start.34 = (bf16[112,768]{1,0:T(8,128)(2,1)}, bf16[112,768]{1,0:T(8,128)(2,1)S(1)}, u32[]{:S(2)}, u32[]{:S(2)}) collective-permute-start(bf16[112,768]{1,0:T(8,128)(2,1)} %get-tuple-element.295), channel_id=1, source_target_pairs={{0,16},{16,0},{1,17},{17,1},{2,18},{18,2},{3,19},{19,3},{4,20},{20... | collective-permute-start | bytes 516104 | tf_op jit(solution)/shard_map/ppermute | solution.py:63
  200.7 15.7 %collective-permute-start.36 = (bf16[512,1536]{1,0:T(8,128)(2,1)}, bf16[512,1536]{1,0:T(8,128)(2,1)S(1)}, u32[]{:S(2)}, u32[]{:S(2)}) collective-permute-start(bf16[512,1536]{1,0:T(8,128)(2,1)} %get-tuple-element.323), channel_id=1, source_target_pairs={{0,16},{16,0},{1,17},{17,1},{2,18},{18,2},{3,19},{19,3},{4,20},{20... | collective-permute-start | bytes 4718600 | tf_op jit(solution)/shard_map/ppermute | solution.py:63
  207.4 11.2 %collective-permute-start.47 = (bf16[8,6528]{1,0:T(8,128)(2,1)}, bf16[8,6528]{1,0:T(8,128)(2,1)S(1)}, u32[]{:S(2)}, u32[]{:S(2)}) collective-permute-start(bf16[8,6528]{1,0:T(8,128)(2,1)} %get-tuple-element.376), channel_id=1, source_target_pairs={{0,16},{16,0},{1,17},{17,1},{2,18},{18,2},{3,19},{19,3},{4,20},{20... | collective-permute-start | bytes 313352 | tf_op jit(solution)/shard_map/ppermute | solution.py:63
  216.5 20.6 %collective-permute-start.37 = (bf16[8,48,768]{2,1,0:T(8,128)(2,1)}, bf16[8,48,768]{2,1,0:T(8,128)(2,1)S(1)}, u32[]{:S(2)}, u32[]{:S(2)}) collective-permute-start(bf16[8,48,768]{2,1,0:T(8,128)(2,1)} %get-tuple-element.325), channel_id=1, source_target_pairs={{0,2},{1,3},{2,0},{3,1},{4,6},{5,7},{6,4},{7,5},{8,10},{9,11},{10,... | collective-permute-start | bytes 1769480 | tf_op jit(solution)/shard_map/ppermute | solution.py:68
  218.4 18.8 %collective-permute-start.38 = (bf16[8,48,768]{2,1,0:T(8,128)(2,1)}, bf16[8,48,768]{2,1,0:T(8,128)(2,1)S(1)}, u32[]{:S(2)}, u32[]{:S(2)}) collective-permute-start(bf16[8,48,768]{2,1,0:T(8,128)(2,1)} %get-tuple-element.327), channel_id=1, source_target_pairs={{0,1},{1,0},{2,3},{3,2},{4,5},{5,4},{6,7},{7,6},{8,9},{9,8},{10,11... | collective-permute-start | bytes 1769480 | tf_op jit(solution)/shard_map/ppermute | solution.py:68
  225.9 41.2 %collective-permute-start.41 = (bf16[8,96,768]{2,1,0:T(8,128)(2,1)}, bf16[8,96,768]{2,1,0:T(8,128)(2,1)S(1)}, u32[]{:S(2)}, u32[]{:S(2)}) collective-permute-start(bf16[8,96,768]{2,1,0:T(8,128)(2,1)} %get-tuple-element.345), channel_id=1, source_target_pairs={{0,2},{1,3},{2,0},{3,1},{4,6},{5,7},{6,4},{7,5},{8,10},{9,11},{10,... | collective-permute-start | bytes 3538952 | tf_op jit(solution)/shard_map/ppermute | solution.py:68
  236.5 26.9 %collective-permute-start.42 = (bf16[8,48,768]{2,1,0:T(8,128)(2,1)}, bf16[8,48,768]{2,1,0:T(8,128)(2,1)S(1)}, u32[]{:S(2)}, u32[]{:S(2)}) collective-permute-start(bf16[8,48,768]{2,1,0:T(8,128)(2,1)} %get-tuple-element.347), channel_id=1, source_target_pairs={{0,1},{1,0},{2,3},{3,2},{4,5},{5,4},{6,7},{7,6},{8,9},{9,8},{10,11... | collective-permute-start | bytes 1769480 | tf_op jit(solution)/shard_map/ppermute | solution.py:68
  237.3 29.8 %collective-permute-start.40 = (bf16[4,48,768]{2,1,0:T(8,128)(2,1)S(1)}, bf16[4,48,768]{2,1,0:T(8,128)(2,1)S(1)}, u32[]{:S(2)}, u32[]{:S(2)}) collective-permute-start(bf16[4,48,768]{2,1,0:T(8,128)(2,1)S(1)} %get-tuple-element.464), channel_id=1, source_target_pairs={{0,2},{1,3},{2,0},{3,1},{4,6},{5,7},{6,4},{7,5},{8,10},{9,11},{10,... | collective-permute-start | bytes 884744 | tf_op jit(solution)/shard_map/ppermute | solution.py:68
  239.3 27.8 %collective-permute-start.39 = (bf16[4,48,768]{2,1,0:T(8,128)(2,1)S(1)}, bf16[4,48,768]{2,1,0:T(8,128)(2,1)S(1)}, u32[]{:S(2)}, u32[]{:S(2)}) collective-permute-start(bf16[4,48,768]{2,1,0:T(8,128)(2,1)S(1)} %get-tuple-element.466), channel_id=1, source_target_pairs={{0,1},{1,0},{2,3},{3,2},{4,5},{5,4},{6,7},{7,6},{8,9},{9,8},{10,11... | collective-permute-start | bytes 884744 | tf_op jit(solution)/shard_map/ppermute | solution.py:68
  267.9 16.2 %collective-permute-start.44 = (bf16[2,512,768]{2,1,0:T(8,128)(2,1)}, bf16[2,512,768]{2,1,0:T(8,128)(2,1)S(1)}, u32[]{:S(2)}, u32[]{:S(2)}) collective-permute-start(bf16[2,512,768]{2,1,0:T(8,128)(2,1)} %get-tuple-element.359), channel_id=1, source_target_pairs={{0,16},{16,0},{1,17},{17,1},{2,18},{18,2},{3,19},{19,3},{4,20},{20... | collective-permute-start | bytes 4718600 | tf_op jit(solution)/shard_map/ppermute | solution.py:63
  269.1 24.7 %collective-permute-start.45 = (bf16[4,96,768]{2,1,0:T(8,128)(2,1)}, bf16[4,96,768]{2,1,0:T(8,128)(2,1)}, u32[]{:S(2)}, u32[]{:S(2)}) collective-permute-start(bf16[4,96,768]{2,1,0:T(8,128)(2,1)} %get-tuple-element.450), channel_id=1, source_target_pairs={{0,1},{1,0},{2,3},{3,2},{4,5},{5,4},{6,7},{7,6},{8,9},{9,8},{10,11... | collective-permute-start | bytes 1769480 | tf_op jit(solution)/shard_map/ppermute | solution.py:68
  271.0 13.2 %collective-permute-start.43 = (bf16[2,96,768]{2,1,0:T(8,128)(2,1)}, bf16[2,96,768]{2,1,0:T(8,128)(2,1)S(1)}, u32[]{:S(2)}, u32[]{:S(2)}) collective-permute-start(bf16[2,96,768]{2,1,0:T(8,128)(2,1)} %get-tuple-element.462), channel_id=1, source_target_pairs={{0,4},{1,5},{2,6},{3,7},{4,0},{5,1},{6,2},{7,3},{8,12},{9,13},{10,... | collective-permute-start | bytes 884744 | tf_op jit(solution)/shard_map/ppermute | solution.py:68
  272.7 21.1 %collective-permute-start.46 = (bf16[4,48,768]{2,1,0:T(8,128)(2,1)}, bf16[4,48,768]{2,1,0:T(8,128)(2,1)}, u32[]{:S(2)}, u32[]{:S(2)}) collective-permute-start(bf16[4,48,768]{2,1,0:T(8,128)(2,1)} %get-tuple-element.460), channel_id=1, source_target_pairs={{0,2},{1,3},{2,0},{3,1},{4,6},{5,7},{6,4},{7,5},{8,10},{9,11},{10,... | collective-permute-start | bytes 884744 | tf_op jit(solution)/shard_map/ppermute | solution.py:68
  294.8 20.8 %collective-permute-start.50 = (bf16[8,48,768]{2,1,0:T(8,128)(2,1)}, bf16[8,48,768]{2,1,0:T(8,128)(2,1)S(1)}, u32[]{:S(2)}, u32[]{:S(2)}) collective-permute-start(bf16[8,48,768]{2,1,0:T(8,128)(2,1)} %get-tuple-element.384), channel_id=1, source_target_pairs={{0,2},{1,3},{2,0},{3,1},{4,6},{5,7},{6,4},{7,5},{8,10},{9,11},{10,... | collective-permute-start | bytes 1769480 | tf_op jit(solution)/shard_map/ppermute | solution.py:68
  296.8 18.9 %collective-permute-start.51 = (bf16[8,48,768]{2,1,0:T(8,128)(2,1)}, bf16[8,48,768]{2,1,0:T(8,128)(2,1)S(1)}, u32[]{:S(2)}, u32[]{:S(2)}) collective-permute-start(bf16[8,48,768]{2,1,0:T(8,128)(2,1)} %get-tuple-element.386), channel_id=1, source_target_pairs={{0,1},{1,0},{2,3},{3,2},{4,5},{5,4},{6,7},{7,6},{8,9},{9,8},{10,11... | collective-permute-start | bytes 1769480 | tf_op jit(solution)/shard_map/ppermute | solution.py:68
  300.0 15.6 %collective-permute-start.52 = (bf16[2,144,768]{2,1,0:T(8,128)(2,1)S(1)}, bf16[2,144,768]{2,1,0:T(8,128)(2,1)S(1)}, u32[]{:S(2)}, u32[]{:S(2)}) collective-permute-start(bf16[2,144,768]{2,1,0:T(8,128)(2,1)S(1)} %get-tuple-element.452), channel_id=1, source_target_pairs={{0,4},{1,5},{2,6},{3,7},{4,0},{5,1},{6,2},{7,3},{8,12},{9,13},{10,... | collective-permute-start | bytes 1327112 | tf_op jit(solution)/shard_map/ppermute | solution.py:68
  301.9 12.7 %collective-permute-start.53 = (bf16[1,96,768]{2,1,0:T(8,128)(2,1)S(1)}, bf16[1,96,768]{2,1,0:T(8,128)(2,1)S(1)}, u32[]{:S(2)}, u32[]{:S(2)}) collective-permute-start(bf16[1,96,768]{2,1,0:T(8,128)(2,1)S(1)} %get-tuple-element.470), channel_id=1, source_target_pairs={{0,8},{1,9},{2,10},{3,11},{4,12},{5,13},{6,14},{7,15},{8,0},{9,1},... | collective-permute-start | bytes 442376 | tf_op jit(solution)/shard_map/ppermute | solution.py:68
  302.8 12.1 %collective-permute-start.54 = (f32[8,768]{1,0:T(8,128)S(1)}, f32[8,768]{1,0:T(8,128)S(1)}, u32[]{:S(2)}, u32[]{:S(2)}) collective-permute-start(f32[8,768]{1,0:T(8,128)S(1)} %add.207), channel_id=1, source_target_pairs={{0,8},{1,9},{2,10},{3,11},{4,12},{5,13},{6,14},{7,15},{8,0},{9,1},... | collective-permute-start | bytes 73736 | tf_op jit(solution)/shard_map/ppermute | solution.py:68
  319.6 18.5 %collective-permute-start.61 = (bf16[1,144,768]{2,1,0:T(8,128)(2,1)}, bf16[1,144,768]{2,1,0:T(8,128)(2,1)S(1)}, u32[]{:S(2)}, u32[]{:S(2)}) collective-permute-start(bf16[1,144,768]{2,1,0:T(8,128)(2,1)} %get-tuple-element.468), channel_id=1, source_target_pairs={{0,8},{1,9},{2,10},{3,11},{4,12},{5,13},{6,14},{7,15},{8,0},{9,1},... | collective-permute-start | bytes 663560 | tf_op jit(solution)/shard_map/ppermute | solution.py:68
  327.0 14.0 %collective-permute-start.60 = (bf16[2,96,768]{2,1,0:T(8,128)(2,1)S(1)}, bf16[2,96,768]{2,1,0:T(8,128)(2,1)S(1)}, u32[]{:S(2)}, u32[]{:S(2)}) collective-permute-start(bf16[2,96,768]{2,1,0:T(8,128)(2,1)S(1)} %get-tuple-element.454), channel_id=1, source_target_pairs={{0,4},{1,5},{2,6},{3,7},{4,0},{5,1},{6,2},{7,3},{8,12},{9,13},{10,... | collective-permute-start | bytes 884744 | tf_op jit(solution)/shard_map/ppermute | solution.py:68
  329.2 14.1 %all-to-all-start.1 = ((bf16[16,8,768]{2,1,0:T(8,128)(2,1)}), bf16[16,8,768]{2,1,0:T(8,128)(2,1)S(1)}, u32[]{:S(2)}, u32[]{:S(2)}) async-start(bf16[16,8,768]{2,1,0:T(8,128)(2,1)} %bitcast.116), calls=%async_computation.1 | async-start | bytes 393216 | tf_op jit(solution)/shard_map/all_to_all | solution.py:1220
  336.9 9.9 %collective-permute-start.64 = (bf16[512,384]{1,0:T(8,128)(2,1)}, bf16[512,384]{1,0:T(8,128)(2,1)S(1)}, u32[]{:S(2)}, u32[]{:S(2)}) collective-permute-start(bf16[512,384]{1,0:T(8,128)(2,1)} %get-tuple-element.416), channel_id=1, source_target_pairs={{0,16},{16,0},{1,17},{17,1},{2,18},{18,2},{3,19},{19,3},{4,20},{20... | collective-permute-start | bytes 1179656 | tf_op jit(solution)/shard_map/ppermute | solution.py:63
  343.4 10.5 %collective-permute-start.68 = (bf16[144,768]{1,0:T(8,128)(2,1)S(1)}, bf16[144,768]{1,0:T(8,128)(2,1)S(1)}, u32[]{:S(2)}, u32[]{:S(2)}) collective-permute-start(bf16[144,768]{1,0:T(8,128)(2,1)S(1)} %get-tuple-element.475), channel_id=1, source_target_pairs={{0,16},{16,0},{1,17},{17,1},{2,18},{18,2},{3,19},{19,3},{4,20},{20... | collective-permute-start | bytes 663560 | tf_op jit(solution)/shard_map/ppermute | solution.py:63
  343.6 9.3 %collective-permute-start.66 = (bf16[1,96,768]{2,1,0:T(8,128)(2,1)S(1)}, bf16[1,96,768]{2,1,0:T(8,128)(2,1)S(1)}, u32[]{:S(2)}, u32[]{:S(2)}) collective-permute-start(bf16[1,96,768]{2,1,0:T(8,128)(2,1)S(1)} %add_convert_fusion.20), channel_id=1, source_target_pairs={{0,8},{1,9},{2,10},{3,11},{4,12},{5,13},{6,14},{7,15},{8,0},{9,1},... | collective-permute-start | bytes 442376 | tf_op jit(solution)/shard_map/ppermute | solution.py:68
  (90 other events, 539.1 us)
Sparse Core Ops, SparseCore 0:
  14.4 131.4 all-gather.4
  219.4 61.9 all-gather.6
